TPU v7x, 32 devices: a whole 2x2x4 slice. The times are simulated.
32 devices in a mesh: prow: 4 (over y, x), pcol: 8 (over z, core).
Axes of the slice: x: 2, y: 2, z: 4, core: 2. Of those that a mesh axis runs over, the one named last changes fastest.
Arguments:
- inverse_panel: float32 [1024, 4, 8, 32], P('prow', None, 'pcol'), may hold values from -6 to 6
- lower_blocks: float32 [4, 8, 32, 2048], P('prow', None, None, 'pcol'), may hold values from -0.25 to 0.25
- diag_inverse: float32 [2048, 128], P('pcol'), may hold values from -6 to 6
- pattern: int32 [8, 16], replicated, may hold values 0 or 1
- widths: int32 [16], replicated, may hold values from 1 to 128, 1536 in all
Outputs:
- selected_rows: float32 [2048, 1024], P('pcol', 'prow')
- diag_block: float32 [2048, 128], P('pcol')
All inputs are finite; a program needn't handle non-finite values.
Results may differ from a plain program's by a relative error of at most 0.00007.
Values sent between devices are 32-bit elements; how exact they have to be, the bound alone decides.
No kernel may reach another device: no remote copies, remote signals or barrier semaphores. Data moves between devices by JAX's collectives and lax.ppermute only.
A program may use at most 128 MiB of HBM per device.

v0:
```python
import jax
import jax.numpy as jnp
from jax import lax
from jax.sharding import PartitionSpec as P


def per_device(inverse_panel, lower_blocks, diag_inverse, pattern, widths):
    row_index = lax.axis_index("prow")
    col_index = lax.axis_index("pcol")
    rows_here = inverse_panel.shape[0]
    run_rows = lower_blocks.shape[2]
    col_width = lower_blocks.shape[3]
    col_count = lower_blocks.shape[1]
    block_len = diag_inverse.shape[1]
    sup_here = col_width // block_len
    block_total = pattern.shape[0]
    global_rows = row_index * rows_here + jnp.arange(rows_here, dtype=jnp.int32)
    onehot = (
        global_rows[:, None] // block_len == jnp.arange(block_total, dtype=jnp.int32)[None, :]
    ).astype(jnp.float32)
    pattern_local = lax.dynamic_slice_in_dim(pattern, col_index * sup_here, sup_here, 1).astype(
        jnp.float32
    )
    row_select = jnp.dot(onehot, pattern_local, preferred_element_type=jnp.float32)
    row_expand = jnp.repeat(row_select, block_len, axis=1)
    widths_local = lax.dynamic_slice_in_dim(widths, col_index * sup_here, sup_here, 0)
    alive = (jnp.arange(block_len, dtype=jnp.int32)[None, :] < widths_local[:, None]).astype(
        jnp.float32
    )
    mask_local = row_expand * alive.reshape(col_width)[None, :]
    lower_cols = lower_blocks.reshape(rows_here, col_width) * mask_local
    lower_four = lower_cols.reshape(1, col_count, run_rows, col_width)
    lower_full = lax.all_gather(lower_four, "prow", axis=0, tiled=True)
    summed = jnp.einsum(
        "iabt,abtk->ki",
        lax.all_gather(inverse_panel, "pcol", axis=2, tiled=True),
        lower_full,
        precision=lax.Precision.HIGHEST,
    )
    trans_out = -summed
    selected = trans_out * mask_local.T
    sel_blocks = selected.reshape(sup_here, block_len, rows_here)
    low_blocks = lower_cols.reshape(rows_here, sup_here, block_len)
    crossed = jnp.einsum("skn,nsj->skj", sel_blocks, low_blocks, precision=lax.Precision.HIGHEST)
    crossed = lax.psum(crossed, "prow")
    both_alive = alive[:, :, None] * alive[:, None, :]
    diag_out = (diag_inverse.reshape(sup_here, block_len, block_len) - crossed) * both_alive
    return (selected, diag_out.reshape(col_width, block_len))


def solution(mesh):
    placed = (
        P("prow", None, "pcol", None),
        P("prow", None, None, "pcol"),
        P("pcol", None),
        P(),
        P(),
    )
    return jax.shard_map(
        per_device,
        mesh=mesh,
        in_specs=placed,
        out_specs=(P("pcol", "prow"), P("pcol", None)),
        check_vma=False,
    )
```

profile of v0, /device:TPU:0, one launch (start us, length us, event | category | flops | bytes accessed | tf_op | source)
XLA Modules:
  0.0 118.1 jit_solution(9628914285847568469)
XLA Ops:
  7.2 0.0 all-gather.3.cloned.1.call-start
  7.2 0.0 copy-start.3
  7.2 0.7 copy-done.3
  7.9 0.3 fusion.6
  8.2 0.1 copy.14
  8.3 0.3 broadcast_in_dim.2.clone
  8.6 0.0 copy-start.4
  8.7 0.0 copy-start
  8.7 0.2 reshape.135
  8.9 0.4 copy-done.4
  9.3 0.1 dynamic_slice.7
  9.4 0.1 compare_convert_fusion
  9.5 0.2 copy-done
  9.6 0.7 multiply_multiply_fusion
  10.4 0.0 all-gather.3.cloned.1.call-update
  10.4 0.0 all-gather.5.cloned.1.call-start
  10.4 0.7 all-gather.5.cloned.1.call-update
  11.1 0.0 all-reduce.2.cloned.1.call-start
  11.2 0.1 bitcast_multiply_fusion
  11.3 0.1 reshape.139
  11.4 28.4 %all-gather.3.cloned.1.call-done = f32[4,8,32,256]{3,2,1,0:T(8,128)} async-done(((f32[1,8,32,256]{3,2,1,0:T(8,128)}), f32[4,8,32,256]{3,2,1,0:T(8,128)}) %all-gather.3.cloned.1.call-update) | async-done | bytes 1048592 | tf_op jit(solution)/shard_map/all_gather | solution.py:33
  39.9 23.7 %all-gather.5.cloned.1.call-done = f32[256,4,8,32]{0,3,2,1:T(8,128)} async-done(((f32[256,4,1,32]{0,3,2,1:T(8,128)}), f32[256,4,8,32]{0,3,2,1:T(8,128)}) %all-gather.5.cloned.1.call-update) | async-done | bytes 1048592 | tf_op jit(solution)/shard_map/all_gather | solution.py:36
  63.6 3.4 %fusion.1 = f32[256,256]{1,0:T(8,128)S(1)} fusion(f32[4,8,32,256]{3,2,1,0:T(8,128)} %all-gather.3.cloned.1.call-done, f32[256,4,8,32]{0,3,2,1:T(8,128)} %all-gather.5.cloned.1.call-done, f32[256,256]{0,1:T(8,128)S(1)} %bitcast_multiply_fusion), kind=kOutput, calls=%fused_computation.2 | convolution fusion | flops 805437440 | bytes 2621440 | tf_op jit(solution)/shard_map/iabt,abtk->ki/dot_general | solution.py:34
  67.0 0.0 copy-start.1
  67.0 1.1 fusion.2
  68.1 0.0 copy-done.1
  68.1 0.0 copy-start.2
  68.1 0.0 all-reduce.2.cloned.1.call-update
  68.1 41.8 %all-reduce.2.cloned.1.call-done = f32[2,128,128]{2,1,0:T(8,128)} async-done(((f32[2,128,128]{2,1,0:T(8,128)}), f32[2,128,128]{2,1,0:T(8,128)}) %all-reduce.2.cloned.1.call-update) | async-done | bytes 131088 | tf_op jit(solution)/shard_map/psum | solution.py:45
  109.9 0.0 copy-done.2
  109.9 1.7 %multiply_multiply_fusion.1 = f32[2,128,128]{2,1,0:T(8,128)} fusion(f32[2,128,128]{2,1,0:T(8,128)S(1)} %bitcast.23, f32[2,128,128]{2,1,0:T(8,128)} %all-reduce.2.cloned.1.call-done, f32[2,128]{1,0:T(2,128)S(1)} %get-tuple-element.2), kind=kLoop, calls=%fused_computation.8 | loop fusion | flops 98304 | bytes 394240 | tf_op jit(solution)/shard_map/mul | solution.py:47
  (1 shorter events, 0.0 us)
Async XLA Ops:
  7.2 32.7 %all-gather.3.cloned.1.call-start = ((), (), s32[]{:S(2)}) async-start(), calls=%async_computation | async-start | bytes 1310720 | tf_op jit(solution)/shard_map/all_gather | solution.py:33
  7.2 0.7 copy-start.3
  8.6 0.7 copy-start.4
  8.7 1.0 copy-start
  10.4 53.2 %all-gather.5.cloned.1.call-start = ((), (), s32[]{:S(2)}) async-start(), calls=%async_computation.1 | async-start | bytes 1179648 | tf_op jit(solution)/shard_map/all_gather | solution.py:36
  11.1 98.8 %all-reduce.2.cloned.1.call-start = ((), (), s32[]{:S(2)}) async-start(), calls=%async_computation.2 | async-start | bytes 262144 | tf_op jit(solution)/shard_map/psum | solution.py:45
  67.0 1.2 copy-start.1
  68.1 41.8 %copy-start.2 = (f32[256,128]{1,0:T(8,128)S(1)}, f32[256,128]{1,0:T(8,128)}, u32[]{:S(2)}) copy-start(f32[256,128]{1,0:T(8,128)} %param.7) | copy-start | bytes 393220
Sparse Core Ops, SparseCore 0:
  10.5 29.3 all-gather.2
  41.5 22.0 all-gather.4
  68.3 41.6 all-reduce.1
where the time goes:
time: 118 us
  waiting for transfers between devices  94.7 us (80%)
  between operations  13.8 us (12%)
  matrix products  4.75 us (4%)
  other arithmetic  2.59 us (2%)
  local copies, waits for them, and re-layouts  2.16 us (2%)
    psum x1, waiting for transfers between devices, per_device(): crossed = lax.psum(crossed, 'prow')  41.8 us
    all_gather x1, waiting for transfers between devices, per_device(): lower_full = lax.all_gather(lower_four, 'prow', axis=0, tiled=True)  28.4 us
    all_gather x1, waiting for transfers between devices, per_device(): lax.all_gather(inverse_panel, 'pcol', axis=2, tiled=True)  23.7 us
    dot_general x1, matrix products, per_device(): jnp.einsum('iabt,abtk->ki', lax.all_gather(inverse_panel, 'pcol', axis=2,...  3.36 us
  transfers between devices with their start and end apart: 3, of which 3 were waited for; matrix products, arithmetic and copies ran while one was open for 0% of the time, Pallas kernels for 0%

commit v1 on v0

v1 whole, which is shorter than its diff:
```python
import functools
import jax
import jax.numpy as jnp
from jax import lax
from jax.experimental import pallas as pl
from jax.experimental.pallas import tpu as pltpu
from jax.sharding import PartitionSpec as P

ROW_STEP = 256
DEPTH_STEP = 1024


def offset_of(order, block):
    total = 0
    for place, bit in enumerate(order):
        if block >> place & 1:
            total ^= bit
    return total


def split(values):
    high = values.astype(jnp.bfloat16)
    return high, (values - high.astype(jnp.float32)).astype(jnp.bfloat16)


def dot3(a, b, dims):
    (a_high, a_low), (b_high, b_low) = a, b
    dot = functools.partial(
        lax.dot_general, dimension_numbers=(dims, ((), ())), preferred_element_type=jnp.float32
    )
    return dot(a_high, b_high) + (dot(a_high, b_low) + dot(a_low, b_high))


def kernel(shape, orders, *refs):
    row_count, col_count, run, block_len, sup_here = shape
    row_orders, col_orders = orders
    panel_refs, refs = refs[:col_count], refs[col_count:]
    lower_refs, refs = refs[:row_count], refs[row_count:]
    pattern_ref, widths_ref, sel_ref, cross_ref, lh, ll, ah, al = refs
    step = pl.program_id(0)
    row = lax.axis_index("prow")
    col = lax.axis_index("pcol")
    core = lax.rem(col, 2)
    rows_here = col_count * run
    sup = col * sup_here
    lanes = lax.broadcasted_iota(jnp.int32, (block_len, block_len), 1)
    subs = lax.broadcasted_iota(jnp.int32, (block_len, block_len), 0)

    @pl.when(step == 0)
    def _():
        for block, ref in enumerate(lower_refs):
            source = row ^ jnp.where(
                core == 0, offset_of(row_orders[0], block), offset_of(row_orders[1], block)
            )

            @pl.loop(0, rows_here // block_len)
            def _(part):
                base = source * rows_here + part * block_len
                base = pl.multiple_of(base, block_len)
                here = pl.multiple_of(part * block_len, block_len)
                for s in range(sup_here):
                    cols = slice(s * block_len, (s + 1) * block_len)
                    kept = jnp.where(
                        pattern_ref[base // block_len, sup + s] != 0, widths_ref[sup + s], 0
                    )
                    values = jnp.where(lanes < kept, ref[pl.ds(here, block_len), cols], 0.0)
                    high, low = split(values)
                    lh[pl.ds(base, block_len), cols] = high
                    ll[pl.ds(base, block_len), cols] = low

    half = col_count // 2
    for number, ref in enumerate(panel_refs):
        block, other = number % half, number // half
        first, second = (offset_of(order, block) for order in col_orders)
        if other:
            source = col ^ 1 ^ jnp.where(core == 0, second, first)
        else:
            source = col ^ jnp.where(core == 0, first, second)
        for i in range(row_count):
            high, low = split(ref[i * run : (i + 1) * run, :])
            base = pl.multiple_of(i * rows_here + source * run, run)
            ah[pl.ds(base, run), :] = high
            al[pl.ds(base, run), :] = low

    width = sup_here * block_len
    total = None
    depth = row_count * rows_here
    chunk = min(depth, DEPTH_STEP)

    def product(base):
        here = pl.ds(base, chunk)
        return dot3((lh[here, :], ll[here, :]), (ah[here, :], al[here, :]), ((0,), (0,)))

    if depth == chunk:
        total = product(0)
    else:
        total = lax.fori_loop(
            0,
            depth // chunk,
            lambda c, acc: acc + product(pl.multiple_of(c * chunk, chunk)),
            jnp.zeros((width, ROW_STEP), jnp.float32),
        )
    mine = row * rows_here + step * ROW_STEP
    for s in range(sup_here):
        cols = slice(s * block_len, (s + 1) * block_len)
        crossed = None
        for part in range(ROW_STEP // block_len):
            piece = total[cols, part * block_len : (part + 1) * block_len]
            base = pl.multiple_of(mine + part * block_len, block_len)
            kept = jnp.where(pattern_ref[base // block_len, sup + s] != 0, widths_ref[sup + s], 0)
            chosen = jnp.where(subs < kept, -piece, 0.0)
            sel_ref[cols, part * block_len : (part + 1) * block_len] = chosen
            here = pl.ds(base, block_len)
            term = dot3(split(chosen), (lh[here, cols], ll[here, cols]), ((1,), (0,)))
            crossed = term if crossed is None else crossed + term

        @pl.when(step == 0)
        def _():
            cross_ref[cols, :] = crossed

        @pl.when(step != 0)
        def _():
            cross_ref[cols, :] += crossed


def per_device(mesh_sizes, inverse_panel, lower_blocks, diag_inverse, pattern, widths):
    row_count, col_count = mesh_sizes
    rows_here, _, _, run = inverse_panel.shape
    width = lower_blocks.shape[3]
    block_len = diag_inverse.shape[1]
    sup_here = width // block_len
    col_index = lax.axis_index("pcol")

    row_bits = [1 << b for b in range(row_count.bit_length() - 1)]
    col_bits = [1 << b for b in range(1, col_count.bit_length() - 1)][::-1]
    row_orders = (row_bits, row_bits[::-1])
    col_orders = (col_bits, col_bits[::-1])

    def send(values, row_steps, col_steps):
        pairs = []
        for r in range(row_count):
            for c in range(col_count):
                target = (r ^ row_steps[c % 2]) * col_count + (c ^ col_steps[c % 2])
                pairs.append((r * col_count + c, target))
        return lax.ppermute(values, ("prow", "pcol"), pairs)

    def along_rows(values, place):
        return send(values, [order[place] for order in row_orders], (0, 0))

    def along_cols(values, place):
        return send(values, (0, 0), [order[place] for order in col_orders])

    def gathered(own, places, move):
        held = [own]
        for place in range(places):
            held = held + [move(values, place) for values in held]
        return held

    panel = jnp.transpose(inverse_panel, (1, 2, 3, 0)).reshape(row_count * run, rows_here)
    lower = lower_blocks.reshape(rows_here, width)
    lowers = gathered(lower, len(row_bits), along_rows)
    panels = gathered(panel, len(col_bits), along_cols)
    panels = panels + [send(values, (0, 0), (1, 1)) for values in panels]

    depth = row_count * rows_here
    smem = pl.BlockSpec(memory_space=pltpu.SMEM)
    flops = 6 * depth * width * rows_here
    selected, crossed = pl.pallas_call(
        functools.partial(
            kernel,
            (row_count, col_count, run, block_len, sup_here),
            (row_orders, col_orders),
        ),
        grid=(rows_here // ROW_STEP,),
        in_specs=[pl.BlockSpec((row_count * run, ROW_STEP), lambda i: (0, i))] * col_count
        + [pl.BlockSpec((rows_here, width), lambda i: (0, 0), pipeline_mode=pl.Buffered(1))]
        * row_count
        + [smem, smem],
        out_specs=[
            pl.BlockSpec((width, ROW_STEP), lambda i: (0, i)),
            pl.BlockSpec((width, block_len), lambda i: (0, 0)),
        ],
        out_shape=[
            jax.ShapeDtypeStruct((width, rows_here), jnp.float32),
            jax.ShapeDtypeStruct((width, block_len), jnp.float32),
        ],
        scratch_shapes=[pltpu.VMEM((depth, width), jnp.bfloat16)] * 2
        + [pltpu.VMEM((depth, ROW_STEP), jnp.bfloat16)] * 2,
        compiler_params=pltpu.CompilerParams(vmem_limit_bytes=56 << 20),
        cost_estimate=pl.CostEstimate(
            flops=flops, bytes_accessed=4 * depth * (width + rows_here), transcendentals=0
        ),
    )(*panels, *lowers, pattern, widths)

    for place in range(len(row_bits)):
        crossed = crossed + along_rows(crossed, place)
    widths_local = lax.dynamic_slice_in_dim(widths, col_index * sup_here, sup_here, 0)
    alive = jnp.arange(block_len, dtype=jnp.int32)[None, :] < widths_local[:, None]
    both_alive = alive[:, :, None] & alive[:, None, :]
    shape = (sup_here, block_len, block_len)
    difference = diag_inverse.reshape(shape) - crossed.reshape(shape)
    diag_out = jnp.where(both_alive, difference, 0.0)
    return selected, diag_out.reshape(width, block_len)


def solution(mesh):
    placed = (
        P("prow", None, "pcol", None),
        P("prow", None, None, "pcol"),
        P("pcol", None),
        P(),
        P(),
    )
    return jax.shard_map(
        functools.partial(per_device, (mesh.shape["prow"], mesh.shape["pcol"])),
        mesh=mesh,
        in_specs=placed,
        out_specs=(P("pcol", "prow"), P("pcol", None)),
        check_vma=False,
    )
```

time: 118 us -> 38.9 us (0.33)
  waiting for transfers between devices: 94.7 us -> 18.7 us
  between operations: 13.8 us -> 0.77 us
  starting transfers between devices: 0.12 us -> 12.3 us
  matrix products: 4.75 us -> 0 us
  Pallas kernels: 0 us -> 3.73 us
    all_gather x2 -> x0, waiting for transfers between devices: 52.2 us -> none  [the longest x1 28.4 us: per_device(): lower_full = lax.all_gather(lower_four, 'prow', axis=0, tiled=True)]
    psum x1 -> x0, waiting for transfers between devices: 41.8 us -> none  [per_device(): crossed = lax.psum(crossed, 'prow')]
    ppermute x0 -> x12, waiting for transfers between devices: none -> 18.7 us  [send(): return lax.ppermute(values, ('prow', 'pcol'), pairs)]
    ppermute x0 -> x12, starting transfers between devices: none -> 12.3 us  [send(): return lax.ppermute(values, ('prow', 'pcol'), pairs)]
    dot_general x3 -> x0, matrix products: 4.75 us -> none  [the longest x1 3.36 us: per_device(): jnp.einsum('iabt,abtk->ki', lax.all_gather(inverse_panel, 'pcol', axis=2,...]
    pallas_call x0 -> x1, Pallas kernels: none -> 3.73 us  [per_device(): pl.pallas_call(functools.partial(kernel, (row_count, col_count, run, bloc...]
    mul x3 -> x0, other arithmetic: 2.51 us -> none  [the longest x1 1.67 us: per_device(): (diag_inverse.reshape(sup_here, block_len, block_len) - crossed) * both_a...]
  transfers between devices with their start and end apart: 3 -> 12, of which waited for: 3 -> 6; matrix products, arithmetic and copies ran while one was open for 0% -> 0% of each run, Pallas kernels for 0% -> 0%
where the time goes in v1:
time: 38.9 us; the launch traced here: 38.7 us
  waiting for transfers between devices  18.7 us (48%)
  starting transfers between devices  12.3 us (32%)
  Pallas kernels  3.73 us (10%)
  other arithmetic  1.75 us (4%)
  local copies, waits for them, and re-layouts  1.45 us (4%)
  between operations  0.77 us (2%)
    ppermute x12, waiting for transfers between devices, send(): return lax.ppermute(values, ('prow', 'pcol'), pairs)  18.7 us
    ppermute x12, starting transfers between devices, send(): return lax.ppermute(values, ('prow', 'pcol'), pairs)  12.3 us
    pallas_call x1, Pallas kernels, per_device(): pl.pallas_call(functools.partial(kernel, (row_count, col_count, run, bloc...  3.73 us
    unnamed x24, local copies, waits for them, and re-layouts  1.38 us
    add x1, other arithmetic, per_device(): crossed = crossed + along_rows(crossed, place)  0.92 us
  transfers between devices with their start and end apart: 12, of which 6 were waited for; matrix products, arithmetic and copies ran while one was open for 0% of the time, Pallas kernels for 0%

profile of v1, /device:TPU:0, one launch (start us, length us, event | category | flops | bytes accessed | tf_op | source)
XLA Modules:
  0.0 38.7 jit_solution(3151625492292754635)
XLA Ops:
  0.6 3.0 %collective-permute-start.7 = (f32[256,256]{1,0:T(8,128)}, f32[256,256]{1,0:T(8,128)S(1)}, u32[]{:S(2)}, u32[]{:S(2)}) collective-permute-start(f32[256,256]{1,0:T(8,128)} %bitcast.10), channel_id=1, source_target_pairs={{0,8},{1,17},{2,10},{3,19},{4,12},{5,21},{6,14},{7,23},{8,0},{9,25... | collective-permute-start | bytes 786440 | tf_op jit(solution)/shard_map/ppermute | solution.py:145
  3.6 2.6 %collective-permute-start = (f32[128,256]{1,0:T(8,128)}, f32[128,256]{1,0:T(8,128)S(1)}, u32[]{:S(2)}, u32[]{:S(2)}) collective-permute-start(f32[128,256]{1,0:T(8,128)} %bitcast.13), channel_id=1, source_target_pairs={{0,4},{1,3},{2,6},{3,1},{4,0},{5,7},{6,2},{7,5},{8,12},{9,11},{10,... | collective-permute-start | bytes 393224 | tf_op jit(solution)/shard_map/ppermute | solution.py:145
  6.2 1.6 %collective-permute-start.1 = (f32[128,256]{1,0:T(8,128)}, f32[128,256]{1,0:T(8,128)S(1)}, u32[]{:S(2)}, u32[]{:S(2)}) collective-permute-start(f32[128,256]{1,0:T(8,128)} %bitcast.14), channel_id=1, source_target_pairs={{0,2},{1,5},{2,0},{3,7},{4,6},{5,1},{6,4},{7,3},{8,10},{9,13},{10,... | collective-permute-start | bytes 393224 | tf_op jit(solution)/shard_map/ppermute | solution.py:145
  7.8 0.0 collective-permute-start.3
  7.8 1.5 %collective-permute-start.8 = (f32[256,256]{1,0:T(8,128)}, f32[256,256]{1,0:T(8,128)S(1)}, u32[]{:S(2)}, u32[]{:S(2)}) collective-permute-start(f32[256,256]{1,0:T(8,128)} %bitcast.11), channel_id=1, source_target_pairs={{0,16},{1,9},{2,18},{3,11},{4,20},{5,13},{6,22},{7,15},{8,24},{9,1... | collective-permute-start | bytes 786440 | tf_op jit(solution)/shard_map/ppermute | solution.py:145
  9.3 6.0 %collective-permute-done.refs_1_ = f32[128,256]{1,0:T(8,128)S(1)} collective-permute-done((f32[128,256]{1,0:T(8,128)}, f32[128,256]{1,0:T(8,128)S(1)}, u32[]{:S(2)}, u32[]{:S(2)}) %collective-permute-start) | collective-permute-done | bytes 131104 | tf_op jit(solution)/shard_map/ppermute | solution.py:145
  15.3 0.0 copy-start.3
  15.3 0.6 %collective-permute-start.2 = (f32[128,256]{1,0:T(8,128)S(1)}, f32[128,256]{1,0:T(8,128)S(1)}, u32[]{:S(2)}, u32[]{:S(2)}) collective-permute-start(f32[128,256]{1,0:T(8,128)S(1)} %collective-permute-done.refs_1_), channel_id=1, source_target_pairs={{0,2},{1,5},{2,0},{3,7},{4,6},{5,1},{6,4},{7,3},{8,10},{9,13},{10,... | collective-permute-start | bytes 393224 | tf_op jit(solution)/shard_map/ppermute | solution.py:145
  15.9 0.0 collective-permute-done.7.refs_9_
  16.0 0.0 copy-start
  16.0 0.6 %collective-permute-start.9 = (f32[256,256]{1,0:T(8,128)S(1)}, f32[256,256]{1,0:T(8,128)S(1)}, u32[]{:S(2)}, u32[]{:S(2)}) collective-permute-start(f32[256,256]{1,0:T(8,128)S(1)} %collective-permute-done.7.refs_9_), channel_id=1, source_target_pairs={{0,16},{1,9},{2,18},{3,11},{4,20},{5,13},{6,22},{7,15},{8,24},{9,1... | collective-permute-start | bytes 786440 | tf_op jit(solution)/shard_map/ppermute | solution.py:145
  16.6 0.0 collective-permute-done.1.refs_2_
  16.6 0.0 collective-permute-start.4
  16.6 0.0 collective-permute-done.3.refs_4_
  16.6 0.0 copy-start.5
  16.6 0.5 %collective-permute-start.5 = (f32[128,256]{1,0:T(8,128)S(1)}, f32[128,256]{1,0:T(8,128)S(1)}, u32[]{:S(2)}, u32[]{:S(2)}) collective-permute-start(f32[128,256]{1,0:T(8,128)S(1)} %collective-permute-done.1.refs_2_), channel_id=1, source_target_pairs={{0,1},{1,0},{2,3},{3,2},{4,5},{5,4},{6,7},{7,6},{8,9},{9,8},{10,11... | collective-permute-start | bytes 393224 | tf_op jit(solution)/shard_map/ppermute | solution.py:145
  17.1 3.2 %collective-permute-done.2.refs_3_ = f32[128,256]{1,0:T(8,128)S(1)} collective-permute-done((f32[128,256]{1,0:T(8,128)S(1)}, f32[128,256]{1,0:T(8,128)S(1)}, u32[]{:S(2)}, u32[]{:S(2)}) %collective-permute-start.2) | collective-permute-done | bytes 131104 | tf_op jit(solution)/shard_map/ppermute | solution.py:145
  20.3 0.0 collective-permute-start.6
  20.3 0.0 collective-permute-done.4.refs_5_
  20.3 0.0 copy-start.7
  20.3 0.0 collective-permute-done.5.refs_6_
  20.3 0.0 copy-start.8
  20.3 0.0 collective-permute-done.8.refs_10_
  20.4 0.0 copy-start.1
  20.4 1.3 %collective-permute-done.6.refs_7_ = f32[128,256]{1,0:T(8,128)S(1)} collective-permute-done((f32[128,256]{1,0:T(8,128)S(1)}, f32[128,256]{1,0:T(8,128)S(1)}, u32[]{:S(2)}, u32[]{:S(2)}) %collective-permute-start.6) | collective-permute-done | bytes 131104 | tf_op jit(solution)/shard_map/ppermute | solution.py:145
  21.7 0.7 %collective-permute-done.9.refs_11_ = f32[256,256]{1,0:T(8,128)S(1)} collective-permute-done((f32[256,256]{1,0:T(8,128)S(1)}, f32[256,256]{1,0:T(8,128)S(1)}, u32[]{:S(2)}, u32[]{:S(2)}) %collective-permute-start.9) | collective-permute-done | bytes 262176 | tf_op jit(solution)/shard_map/ppermute | solution.py:145
  22.3 0.0 copy-done.3
  22.3 0.0 copy-done
  22.3 0.0 copy-done.4
  22.3 0.0 copy-done.5
  22.3 0.0 copy-done.6
  22.4 0.0 copy-done.7
  22.4 0.0 copy-done.8
  22.4 0.0 copy-done.1
  22.4 0.0 copy-done.9
  22.4 0.0 copy-start.2
  22.4 0.7 %copy-done.2 = f32[256,256]{1,0:T(8,128)} copy-done((f32[256,256]{1,0:T(8,128)}, f32[256,256]{1,0:T(8,128)S(1)}, u32[]{:S(2)}) %copy-start.2) | copy-done | bytes 262168
  23.1 3.7 %shard_map.68 = (f32[256,256]{1,0:T(8,128)}, f32[256,128]{1,0:T(8,128)}) custom-call(f32[128,256]{1,0:T(8,128)} %bitcast.16, f32[128,256]{1,0:T(8,128)} %copy-done.3, f32[128,256]{1,0:T(8,128)} %copy-done.4, f32[128,256]{1,0:T(8,128)} %copy-done.6, f32[128,256]{1,0:T(8,128)} %copy-done.5, f32[128,256]{1,0:T(8,128)} %copy-done.7, f32[128,256]{1,0:T(8,128)} %copy-done.8, ...), custom_call_target="tpu_custom_call" | custom-call | flops 402653184 | bytes 2097152 | tf_op jit(solution)/shard_map/pallas_call | solution.py:168
  26.8 0.8 %collective-permute-start.10 = (f32[256,128]{1,0:T(8,128)}, f32[256,128]{1,0:T(8,128)S(1)}, u32[]{:S(2)}, u32[]{:S(2)}) collective-permute-start(f32[256,128]{1,0:T(8,128)} %get-tuple-element.5), channel_id=1, source_target_pairs={{0,8},{1,17},{2,10},{3,19},{4,12},{5,21},{6,14},{7,23},{8,0},{9,25... | collective-permute-start | bytes 393224 | tf_op jit(solution)/shard_map/ppermute | solution.py:145
  27.6 0.7 %copy-done.11 = s32[16]{0:T(128)S(1)} copy-done((s32[16]{0:T(128)S(1)}, s32[16]{0:T(128)}, u32[]{:S(2)}) %copy-start.11) | copy-done | bytes 88
  28.3 0.1 dynamic_slice.3
  28.3 3.7 %collective-permute-done.10 = f32[256,128]{1,0:T(8,128)S(1)} collective-permute-done((f32[256,128]{1,0:T(8,128)}, f32[256,128]{1,0:T(8,128)S(1)}, u32[]{:S(2)}, u32[]{:S(2)}) %collective-permute-start.10) | collective-permute-done | bytes 131104 | tf_op jit(solution)/shard_map/ppermute | solution.py:145
  32.0 0.9 %add.10 = f32[256,128]{1,0:T(8,128)S(1)} add(f32[256,128]{1,0:T(8,128)} %get-tuple-element.5, f32[256,128]{1,0:T(8,128)S(1)} %collective-permute-done.10) | non-fusion elementwise | flops 32768 | bytes 393216 | tf_op jit(solution)/shard_map/add | solution.py:196
  32.9 1.1 %collective-permute-start.11 = (f32[256,128]{1,0:T(8,128)S(1)}, f32[256,128]{1,0:T(8,128)S(1)}, u32[]{:S(2)}, u32[]{:S(2)}) collective-permute-start(f32[256,128]{1,0:T(8,128)S(1)} %add.10), channel_id=1, source_target_pairs={{0,16},{1,9},{2,18},{3,11},{4,20},{5,13},{6,22},{7,15},{8,24},{9,1... | collective-permute-start | bytes 393224 | tf_op jit(solution)/shard_map/ppermute | solution.py:145
  34.0 0.1 iota_compare_fusion
  34.1 3.9 %collective-permute-done.11 = f32[256,128]{1,0:T(8,128)S(1)} collective-permute-done((f32[256,128]{1,0:T(8,128)S(1)}, f32[256,128]{1,0:T(8,128)S(1)}, u32[]{:S(2)}, u32[]{:S(2)}) %collective-permute-start.11) | collective-permute-done | bytes 131104 | tf_op jit(solution)/shard_map/ppermute | solution.py:145
  38.0 0.0 copy-done.10
  38.0 0.8 %subtract_select_fusion = f32[256,128]{1,0:T(8,128)} fusion(f32[256,128]{1,0:T(8,128)S(1)} %copy-done.10, f32[256,128]{1,0:T(8,128)S(1)} %add.10, f32[256,128]{1,0:T(8,128)S(1)} %collective-permute-done.11, pred[256]{0:T(512)(128)(4,1)S(1)} %get-tuple-element.7, pred[2,128]{1,0:T(4,128)(4,1)S(1)} %get-tuple-element.6), kind=kLoop, calls=%fused_computation | loop fusion | flops 131072 | bytes 524800 | tf_op jit(solution)/shard_map/jit(_where)/select_n | solution.py:202
  (5 shorter events, 0.0 us)
Async XLA Ops:
  0.6 15.3 %collective-permute-start.7 = (f32[256,256]{1,0:T(8,128)}, f32[256,256]{1,0:T(8,128)S(1)}, u32[]{:S(2)}, u32[]{:S(2)}) collective-permute-start(f32[256,256]{1,0:T(8,128)} %bitcast.10), channel_id=1, source_target_pairs={{0,8},{1,17},{2,10},{3,19},{4,12},{5,21},{6,14},{7,23},{8,0},{9,25... | collective-permute-start | bytes 786440 | tf_op jit(solution)/shard_map/ppermute | solution.py:145
  3.6 11.7 %collective-permute-start = (f32[128,256]{1,0:T(8,128)}, f32[128,256]{1,0:T(8,128)S(1)}, u32[]{:S(2)}, u32[]{:S(2)}) collective-permute-start(f32[128,256]{1,0:T(8,128)} %bitcast.13), channel_id=1, source_target_pairs={{0,4},{1,3},{2,6},{3,1},{4,0},{5,7},{6,2},{7,5},{8,12},{9,11},{10,... | collective-permute-start | bytes 393224 | tf_op jit(solution)/shard_map/ppermute | solution.py:145
  6.2 10.3 %collective-permute-start.1 = (f32[128,256]{1,0:T(8,128)}, f32[128,256]{1,0:T(8,128)S(1)}, u32[]{:S(2)}, u32[]{:S(2)}) collective-permute-start(f32[128,256]{1,0:T(8,128)} %bitcast.14), channel_id=1, source_target_pairs={{0,2},{1,5},{2,0},{3,7},{4,6},{5,1},{6,4},{7,3},{8,10},{9,13},{10,... | collective-permute-start | bytes 393224 | tf_op jit(solution)/shard_map/ppermute | solution.py:145
  7.8 8.8 %collective-permute-start.3 = (f32[128,256]{1,0:T(8,128)}, f32[128,256]{1,0:T(8,128)S(1)}, u32[]{:S(2)}, u32[]{:S(2)}) collective-permute-start(f32[128,256]{1,0:T(8,128)} %bitcast.15), channel_id=1, source_target_pairs={{0,1},{1,0},{2,3},{3,2},{4,5},{5,4},{6,7},{7,6},{8,9},{9,8},{10,11... | collective-permute-start | bytes 393224 | tf_op jit(solution)/shard_map/ppermute | solution.py:145
  7.8 12.5 %collective-permute-start.8 = (f32[256,256]{1,0:T(8,128)}, f32[256,256]{1,0:T(8,128)S(1)}, u32[]{:S(2)}, u32[]{:S(2)}) collective-permute-start(f32[256,256]{1,0:T(8,128)} %bitcast.11), channel_id=1, source_target_pairs={{0,16},{1,9},{2,18},{3,11},{4,20},{5,13},{6,22},{7,15},{8,24},{9,1... | collective-permute-start | bytes 786440 | tf_op jit(solution)/shard_map/ppermute | solution.py:145
  15.3 7.0 %copy-start.3 = (f32[128,256]{1,0:T(8,128)}, f32[128,256]{1,0:T(8,128)S(1)}, u32[]{:S(2)}) copy-start(f32[128,256]{1,0:T(8,128)S(1)} %collective-permute-done.refs_1_) | copy-start | bytes 393220
  15.3 5.0 %collective-permute-start.2 = (f32[128,256]{1,0:T(8,128)S(1)}, f32[128,256]{1,0:T(8,128)S(1)}, u32[]{:S(2)}, u32[]{:S(2)}) collective-permute-start(f32[128,256]{1,0:T(8,128)S(1)} %collective-permute-done.refs_1_), channel_id=1, source_target_pairs={{0,2},{1,5},{2,0},{3,7},{4,6},{5,1},{6,4},{7,3},{8,10},{9,13},{10,... | collective-permute-start | bytes 393224 | tf_op jit(solution)/shard_map/ppermute | solution.py:145
  16.0 6.4 %copy-start = (f32[256,256]{1,0:T(8,128)}, f32[256,256]{1,0:T(8,128)S(1)}, u32[]{:S(2)}) copy-start(f32[256,256]{1,0:T(8,128)S(1)} %collective-permute-done.7.refs_9_) | copy-start | bytes 786436
  16.0 6.4 %collective-permute-start.9 = (f32[256,256]{1,0:T(8,128)S(1)}, f32[256,256]{1,0:T(8,128)S(1)}, u32[]{:S(2)}, u32[]{:S(2)}) collective-permute-start(f32[256,256]{1,0:T(8,128)S(1)} %collective-permute-done.7.refs_9_), channel_id=1, source_target_pairs={{0,16},{1,9},{2,18},{3,11},{4,20},{5,13},{6,22},{7,15},{8,24},{9,1... | collective-permute-start | bytes 786440 | tf_op jit(solution)/shard_map/ppermute | solution.py:145
  16.6 5.8 %copy-start.4 = (f32[128,256]{1,0:T(8,128)}, f32[128,256]{1,0:T(8,128)S(1)}, u32[]{:S(2)}) copy-start(f32[128,256]{1,0:T(8,128)S(1)} %collective-permute-done.1.refs_2_) | copy-start | bytes 393220
  16.6 3.7 %collective-permute-start.4 = (f32[128,256]{1,0:T(8,128)S(1)}, f32[128,256]{1,0:T(8,128)S(1)}, u32[]{:S(2)}, u32[]{:S(2)}) collective-permute-start(f32[128,256]{1,0:T(8,128)S(1)} %collective-permute-done.refs_1_), channel_id=1, source_target_pairs={{0,1},{1,0},{2,3},{3,2},{4,5},{5,4},{6,7},{7,6},{8,9},{9,8},{10,11... | collective-permute-start | bytes 393224 | tf_op jit(solution)/shard_map/ppermute | solution.py:145
  16.6 5.8 %copy-start.5 = (f32[128,256]{1,0:T(8,128)}, f32[128,256]{1,0:T(8,128)S(1)}, u32[]{:S(2)}) copy-start(f32[128,256]{1,0:T(8,128)S(1)} %collective-permute-done.3.refs_4_) | copy-start | bytes 393220
  16.6 3.7 %collective-permute-start.5 = (f32[128,256]{1,0:T(8,128)S(1)}, f32[128,256]{1,0:T(8,128)S(1)}, u32[]{:S(2)}, u32[]{:S(2)}) collective-permute-start(f32[128,256]{1,0:T(8,128)S(1)} %collective-permute-done.1.refs_2_), channel_id=1, source_target_pairs={{0,1},{1,0},{2,3},{3,2},{4,5},{5,4},{6,7},{7,6},{8,9},{9,8},{10,11... | collective-permute-start | bytes 393224 | tf_op jit(solution)/shard_map/ppermute | solution.py:145
  20.3 2.1 %copy-start.6 = (f32[128,256]{1,0:T(8,128)}, f32[128,256]{1,0:T(8,128)S(1)}, u32[]{:S(2)}) copy-start(f32[128,256]{1,0:T(8,128)S(1)} %collective-permute-done.2.refs_3_) | copy-start | bytes 393220
  20.3 1.3 %collective-permute-start.6 = (f32[128,256]{1,0:T(8,128)S(1)}, f32[128,256]{1,0:T(8,128)S(1)}, u32[]{:S(2)}, u32[]{:S(2)}) collective-permute-start(f32[128,256]{1,0:T(8,128)S(1)} %collective-permute-done.2.refs_3_), channel_id=1, source_target_pairs={{0,1},{1,0},{2,3},{3,2},{4,5},{5,4},{6,7},{7,6},{8,9},{9,8},{10,11... | collective-permute-start | bytes 393224 | tf_op jit(solution)/shard_map/ppermute | solution.py:145
  20.3 2.0 %copy-start.7 = (f32[128,256]{1,0:T(8,128)}, f32[128,256]{1,0:T(8,128)S(1)}, u32[]{:S(2)}) copy-start(f32[128,256]{1,0:T(8,128)S(1)} %collective-permute-done.4.refs_5_) | copy-start | bytes 393220
  20.3 2.0 %copy-start.8 = (f32[128,256]{1,0:T(8,128)}, f32[128,256]{1,0:T(8,128)S(1)}, u32[]{:S(2)}) copy-start(f32[128,256]{1,0:T(8,128)S(1)} %collective-permute-done.5.refs_6_) | copy-start | bytes 393220
  20.4 2.0 %copy-start.1 = (f32[256,256]{1,0:T(8,128)}, f32[256,256]{1,0:T(8,128)S(1)}, u32[]{:S(2)}) copy-start(f32[256,256]{1,0:T(8,128)S(1)} %collective-permute-done.8.refs_10_) | copy-start | bytes 786436
  21.6 0.7 %copy-start.9 = (f32[128,256]{1,0:T(8,128)}, f32[128,256]{1,0:T(8,128)S(1)}, u32[]{:S(2)}) copy-start(f32[128,256]{1,0:T(8,128)S(1)} %collective-permute-done.6.refs_7_) | copy-start | bytes 393220
  22.4 0.7 %copy-start.2 = (f32[256,256]{1,0:T(8,128)}, f32[256,256]{1,0:T(8,128)S(1)}, u32[]{:S(2)}) copy-start(f32[256,256]{1,0:T(8,128)S(1)} %collective-permute-done.9.refs_11_) | copy-start | bytes 786436
  26.8 5.2 %collective-permute-start.10 = (f32[256,128]{1,0:T(8,128)}, f32[256,128]{1,0:T(8,128)S(1)}, u32[]{:S(2)}, u32[]{:S(2)}) collective-permute-start(f32[256,128]{1,0:T(8,128)} %get-tuple-element.5), channel_id=1, source_target_pairs={{0,8},{1,17},{2,10},{3,19},{4,12},{5,21},{6,14},{7,23},{8,0},{9,25... | collective-permute-start | bytes 393224 | tf_op jit(solution)/shard_map/ppermute | solution.py:145
  27.6 0.7 %copy-start.11 = (s32[16]{0:T(128)S(1)}, s32[16]{0:T(128)}, u32[]{:S(2)}) copy-start(s32[16]{0:T(128)} %refs_13_.1) | copy-start | bytes 196
  28.3 9.6 %copy-start.10 = (f32[256,128]{1,0:T(8,128)S(1)}, f32[256,128]{1,0:T(8,128)}, u32[]{:S(2)}) copy-start(f32[256,128]{1,0:T(8,128)} %param.7) | copy-start | bytes 393220
  32.9 5.0 %collective-permute-start.11 = (f32[256,128]{1,0:T(8,128)S(1)}, f32[256,128]{1,0:T(8,128)S(1)}, u32[]{:S(2)}, u32[]{:S(2)}) collective-permute-start(f32[256,128]{1,0:T(8,128)S(1)} %add.10), channel_id=1, source_target_pairs={{0,16},{1,9},{2,18},{3,11},{4,20},{5,13},{6,22},{7,15},{8,24},{9,1... | collective-permute-start | bytes 393224 | tf_op jit(solution)/shard_map/ppermute | solution.py:145

commit v2 on v1

v2 whole, which is shorter than its diff:
```python
import functools
import jax
import jax.numpy as jnp
from jax import lax
from jax.experimental import pallas as pl
from jax.experimental.pallas import tpu as pltpu
from jax.sharding import PartitionSpec as P

ROW_STEP = 256


def offset_of(order, block):
    total = 0
    for place, bit in enumerate(order):
        if block >> place & 1:
            total ^= bit
    return total


def split(values):
    high = values.astype(jnp.bfloat16)
    return high, (values - high.astype(jnp.float32)).astype(jnp.bfloat16)


def dot3(a, b, dims):
    (a_high, a_low), (b_high, b_low) = a, b
    dot = functools.partial(
        lax.dot_general, dimension_numbers=(dims, ((), ())), preferred_element_type=jnp.float32
    )
    return dot(a_high, b_high) + (dot(a_high, b_low) + dot(a_low, b_high))


def kept_columns(pattern_ref, widths_ref, row_block, sup):
    return jnp.where(pattern_ref[row_block, sup] != 0, widths_ref[sup], 0)


def rows_of_pair(ref, source, run, rows_here, row_count):
    pieces = []
    for column in (source, source ^ 1):
        for i in range(row_count):
            base = pl.multiple_of(i * rows_here + column * run, run)
            pieces.append(ref[pl.ds(base, run), :])
    return jnp.concatenate(pieces, axis=0)


def pair_product(lowers, own_ref, other_ref):
    panel = split(jnp.concatenate([own_ref[...], other_ref[...]], axis=0))
    return dot3(lowers, panel, ((0,), (0,)))


def early_kernel(shape, row_orders, col_offsets, *refs):
    row_count, col_count, run, block_len, sup_here = shape
    half = col_count // 2
    panel_refs, refs = refs[: 2 * (half - 1)], refs[2 * (half - 1) :]
    lower_refs, refs = refs[:row_count], refs[row_count:]
    pattern_ref, widths_ref, total_ref, lx_high, lx_low, lm_high, lm_low, lh, ll = refs
    row = lax.axis_index("prow")
    col = lax.axis_index("pcol")
    core = lax.rem(col, 2)
    rows_here = col_count * run
    sup = col * sup_here
    lanes = lax.broadcasted_iota(jnp.int32, (block_len, block_len), 1)

    @pl.when(pl.program_id(0) == 0)
    def _():
        for block, ref in enumerate(lower_refs):
            first, second = (offset_of(order, block) for order in row_orders)
            source = row ^ jnp.where(core == 0, first, second)
            for part in range(rows_here // block_len):
                base = pl.multiple_of(source * rows_here + part * block_len, block_len)
                here = slice(part * block_len, (part + 1) * block_len)
                for s in range(sup_here):
                    cols = slice(s * block_len, (s + 1) * block_len)
                    kept = kept_columns(pattern_ref, widths_ref, base // block_len, sup + s)
                    high, low = split(jnp.where(lanes < kept, ref[here, cols], 0.0))
                    lh[pl.ds(base, block_len), cols] = high
                    ll[pl.ds(base, block_len), cols] = low
                    if block == 0:
                        lm_high[here, cols] = high
                        lm_low[here, cols] = low
        late = col ^ col_offsets[-1]
        lx_high[...] = rows_of_pair(lh, late, run, rows_here, row_count)
        lx_low[...] = rows_of_pair(ll, late, run, rows_here, row_count)

    total = None
    for block in range(half - 1):
        source = col ^ col_offsets[block]
        lowers = tuple(rows_of_pair(ref, source, run, rows_here, row_count) for ref in (lh, ll))
        part = pair_product(lowers, panel_refs[2 * block], panel_refs[2 * block + 1])
        total = part if total is None else total + part
    total_ref[...] = total


def late_kernel(shape, *refs):
    row_count, col_count, run, block_len, sup_here = shape
    total_ref, lx_high, lx_low, lm_high, lm_low, own_ref, other_ref, *refs = refs
    pattern_ref, widths_ref, sel_ref, cross_ref = refs
    step = pl.program_id(0)
    row = lax.axis_index("prow")
    rows_here = col_count * run
    sup = lax.axis_index("pcol") * sup_here
    subs = lax.broadcasted_iota(jnp.int32, (block_len, block_len), 0)
    total = total_ref[...] + pair_product((lx_high[...], lx_low[...]), own_ref, other_ref)
    first = (row * rows_here + step * ROW_STEP) // block_len
    for s in range(sup_here):
        cols = slice(s * block_len, (s + 1) * block_len)
        chosen = []
        for part in range(ROW_STEP // block_len):
            kept = kept_columns(pattern_ref, widths_ref, first + part, sup + s)
            piece = total[cols, part * block_len : (part + 1) * block_len]
            chosen.append(jnp.where(subs < kept, -piece, 0.0))
        chosen = jnp.concatenate(chosen, axis=1)
        sel_ref[cols, :] = chosen
        crossed = dot3(split(chosen), (lm_high[:, cols], lm_low[:, cols]), ((1,), (0,)))

        @pl.when(step == 0)
        def _():
            cross_ref[cols, :] = crossed

        @pl.when(step != 0)
        def _():
            cross_ref[cols, :] += crossed


def per_device(mesh_sizes, inverse_panel, lower_blocks, diag_inverse, pattern, widths):
    row_count, col_count = mesh_sizes
    rows_here, _, _, run = inverse_panel.shape
    width = lower_blocks.shape[3]
    block_len = diag_inverse.shape[1]
    sup_here = width // block_len
    half = col_count // 2
    depth = row_count * rows_here
    col_index = lax.axis_index("pcol")

    row_bits = [1 << b for b in range(row_count.bit_length() - 1)]
    col_bits = [1 << b for b in range(1, col_count.bit_length() - 1)][::-1]
    row_orders = (row_bits, row_bits[::-1])

    def send(values, row_steps, col_step):
        pairs = []
        for r in range(row_count):
            for c in range(col_count):
                target = (r ^ row_steps[c % 2]) * col_count + (c ^ col_step)
                pairs.append((r * col_count + c, target))
        return lax.ppermute(values, ("prow", "pcol"), pairs)

    def along_rows(values, place):
        return send(values, [order[place] for order in row_orders], 0)

    def along_cols(values, place):
        return send(values, (0, 0), col_bits[place])

    def gathered(own, places, move):
        held = [own]
        for place in range(places):
            held = held + [move(values, place) for values in held]
        return held

    panel = jnp.transpose(inverse_panel, (1, 2, 3, 0)).reshape(row_count * run, rows_here)
    lower = lower_blocks.reshape(rows_here, width)
    lowers = gathered(lower, len(row_bits), along_rows)
    panels = gathered(panel, len(col_bits), along_cols)
    panels = [v for values in panels for v in (values, send(values, (0, 0), 1))]
    col_offsets = [offset_of(col_bits, block) for block in range(half)]

    shape = (row_count, col_count, run, block_len, sup_here)
    grid = (rows_here // ROW_STEP,)
    smem = pl.BlockSpec(memory_space=pltpu.SMEM)
    tall = row_count * run
    panel_spec = pl.BlockSpec((tall, ROW_STEP), lambda i: (0, i))
    total_spec = pl.BlockSpec((width, ROW_STEP), lambda i: (0, i))
    pair_spec = pl.BlockSpec((2 * tall, width), lambda i: (0, 0))
    early_bytes = 8 * depth * ROW_STEP + 8 * depth * width + 16 * rows_here * width
    total, *lower_parts = pl.pallas_call(
        functools.partial(early_kernel, shape, row_orders, col_offsets),
        grid=grid,
        in_specs=[panel_spec] * (2 * half - 2)
        + [pl.BlockSpec((rows_here, width), lambda i: (0, 0), pipeline_mode=pl.Buffered(1))]
        * row_count
        + [smem, smem],
        out_specs=[total_spec, pair_spec, pair_spec]
        + [pl.BlockSpec((rows_here, width), lambda i: (0, 0))] * 2,
        out_shape=[jax.ShapeDtypeStruct((width, rows_here), jnp.float32)]
        + [jax.ShapeDtypeStruct((2 * tall, width), jnp.bfloat16)] * 2
        + [jax.ShapeDtypeStruct((rows_here, width), jnp.bfloat16)] * 2,
        scratch_shapes=[pltpu.VMEM((depth, width), jnp.bfloat16)] * 2,
        compiler_params=pltpu.CompilerParams(vmem_limit_bytes=early_bytes + (6 << 20)),
        cost_estimate=pl.CostEstimate(
            flops=6 * depth * width * rows_here, bytes_accessed=8 << 20, transcendentals=0
        ),
    )(*panels[:-2], *lowers, pattern, widths)
    selected, crossed = pl.pallas_call(
        functools.partial(late_kernel, shape),
        grid=grid,
        in_specs=[total_spec, pair_spec, pair_spec]
        + [pl.BlockSpec((ROW_STEP, width), lambda i: (i, 0))] * 2
        + [panel_spec, panel_spec, smem, smem],
        out_specs=[total_spec, pl.BlockSpec((width, block_len), lambda i: (0, 0))],
        out_shape=[
            jax.ShapeDtypeStruct((width, rows_here), jnp.float32),
            jax.ShapeDtypeStruct((width, block_len), jnp.float32),
        ],
        compiler_params=pltpu.CompilerParams(vmem_limit_bytes=12 << 20),
    )(total, *lower_parts, *panels[-2:], pattern, widths)

    arrived = [send(crossed, (block, block), 0) for block in range(1, row_count)][::-1]
    for values in arrived:
        crossed = crossed + values
    widths_local = lax.dynamic_slice_in_dim(widths, col_index * sup_here, sup_here, 0)
    alive = jnp.arange(block_len, dtype=jnp.int32)[None, :] < widths_local[:, None]
    both_alive = alive[:, :, None] & alive[:, None, :]
    blocks = (sup_here, block_len, block_len)
    difference = diag_inverse.reshape(blocks) - crossed.reshape(blocks)
    diag_out = jnp.where(both_alive, difference, 0.0)
    return selected, diag_out.reshape(width, block_len)


def solution(mesh):
    placed = (
        P("prow", None, "pcol", None),
        P("prow", None, None, "pcol"),
        P("pcol", None),
        P(),
        P(),
    )
    return jax.shard_map(
        functools.partial(per_device, (mesh.shape["prow"], mesh.shape["pcol"])),
        mesh=mesh,
        in_specs=placed,
        out_specs=(P("pcol", "prow"), P("pcol", None)),
        check_vma=False,
    )
```

time: 38.9 us -> 34 us (0.87)
  waiting for transfers between devices: 18.7 us -> 12.2 us
  starting transfers between devices: 12.3 us -> 14.3 us
  local copies, waits for them, and re-layouts: 1.45 us -> 2.6 us
  other arithmetic: 1.75 us -> 0.84 us
  Pallas kernels: 3.73 us -> 3.15 us
    ppermute x12 -> x13, waiting for transfers between devices: 18.7 us -> 12.2 us  [send(): return lax.ppermute(values, ('prow', 'pcol'), pairs)]
    ppermute x12 -> x13, starting transfers between devices: 12.3 us -> 14.3 us  [send(): return lax.ppermute(values, ('prow', 'pcol'), pairs)]
    unnamed x24 -> x10, local copies, waits for them, and re-layouts: 1.38 us -> 2.53 us
    add x1 -> x0, other arithmetic: 0.92 us -> none  [per_device(): crossed = crossed + along_rows(crossed, place)]
    pallas_call x1 -> x2, Pallas kernels: 3.73 us -> 3.15 us  [the longest x1 1.7 us: per_device(): pl.pallas_call(functools.partial(late_kernel, shape), grid=grid, in_specs...]
  transfers between devices with their start and end apart: 12 -> 13, of which waited for: 6 -> 4; matrix products, arithmetic and copies ran while one was open for 0% -> 0% of each run, Pallas kernels for 0% -> 4%
where the time goes in v2:
time: 34 us; the launch traced here: 33.8 us
  starting transfers between devices  14.3 us (42%)
  waiting for transfers between devices  12.2 us (36%)
  Pallas kernels  3.15 us (9%)
  local copies, waits for them, and re-layouts  2.6 us (8%)
  other arithmetic  0.84 us (2%)
  between operations  0.7 us (2%)
    ppermute x13, starting transfers between devices, send(): return lax.ppermute(values, ('prow', 'pcol'), pairs)  14.3 us
    ppermute x13, waiting for transfers between devices, send(): return lax.ppermute(values, ('prow', 'pcol'), pairs)  12.2 us
    unnamed x10, local copies, waits for them, and re-layouts  2.53 us
    pallas_call x1, Pallas kernels, per_device(): pl.pallas_call(functools.partial(late_kernel, shape), grid=grid, in_specs...  1.7 us
    pallas_call x1, Pallas kernels, per_device(): pl.pallas_call(functools.partial(early_kernel, shape, row_orders, col_off...  1.45 us
    select_n x1, other arithmetic, per_device(): diag_out = jnp.where(both_alive, difference, 0.0)  0.76 us
  transfers between devices with their start and end apart: 13, of which 4 were waited for; matrix products, arithmetic and copies ran while one was open for 0% of the time, Pallas kernels for 4%

profile of v2, /device:TPU:0, one launch (start us, length us, event | category | flops | bytes accessed | tf_op | source)
XLA Modules:
  0.0 33.8 jit_solution(3342266662635461277)
XLA Ops:
  0.6 3.0 %collective-permute-start.5 = (f32[256,256]{1,0:T(8,128)}, f32[256,256]{1,0:T(8,128)S(1)}, u32[]{:S(2)}, u32[]{:S(2)}) collective-permute-start(f32[256,256]{1,0:T(8,128)} %bitcast.10), channel_id=1, source_target_pairs={{0,8},{1,17},{2,10},{3,19},{4,12},{5,21},{6,14},{7,23},{8,0},{9,25... | collective-permute-start | bytes 786440 | tf_op jit(solution)/shard_map/ppermute | solution.py:145
  3.6 2.6 %collective-permute-start.1 = (f32[128,256]{1,0:T(8,128)}, f32[128,256]{1,0:T(8,128)S(1)}, u32[]{:S(2)}, u32[]{:S(2)}) collective-permute-start(f32[128,256]{1,0:T(8,128)} %bitcast.13), channel_id=1, source_target_pairs={{0,4},{1,5},{2,6},{3,7},{4,0},{5,1},{6,2},{7,3},{8,12},{9,13},{10,... | collective-permute-start | bytes 393224 | tf_op jit(solution)/shard_map/ppermute | solution.py:145
  6.2 1.6 %collective-permute-start.3 = (f32[128,256]{1,0:T(8,128)}, f32[128,256]{1,0:T(8,128)S(1)}, u32[]{:S(2)}, u32[]{:S(2)}) collective-permute-start(f32[128,256]{1,0:T(8,128)} %bitcast.14), channel_id=1, source_target_pairs={{0,2},{1,3},{2,0},{3,1},{4,6},{5,7},{6,4},{7,5},{8,10},{9,11},{10,... | collective-permute-start | bytes 393224 | tf_op jit(solution)/shard_map/ppermute | solution.py:145
  7.8 0.0 collective-permute-start
  7.8 1.5 %collective-permute-start.6 = (f32[256,256]{1,0:T(8,128)}, f32[256,256]{1,0:T(8,128)S(1)}, u32[]{:S(2)}, u32[]{:S(2)}) collective-permute-start(f32[256,256]{1,0:T(8,128)} %bitcast.11), channel_id=1, source_target_pairs={{0,16},{1,9},{2,18},{3,11},{4,20},{5,13},{6,22},{7,15},{8,24},{9,1... | collective-permute-start | bytes 786440 | tf_op jit(solution)/shard_map/ppermute | solution.py:145
  9.3 0.0 collective-permute-done.5.refs_7_
  9.3 0.9 %collective-permute-start.7 = (f32[256,256]{1,0:T(8,128)S(1)}, f32[256,256]{1,0:T(8,128)S(1)}, u32[]{:S(2)}, u32[]{:S(2)}) collective-permute-start(f32[256,256]{1,0:T(8,128)S(1)} %collective-permute-done.5.refs_7_), channel_id=1, source_target_pairs={{0,16},{1,9},{2,18},{3,11},{4,20},{5,13},{6,22},{7,15},{8,24},{9,1... | collective-permute-start | bytes 786440 | tf_op jit(solution)/shard_map/ppermute | solution.py:145
  10.2 2.4 %collective-permute-done.1.refs_2_ = f32[128,256]{1,0:T(8,128)S(1)} collective-permute-done((f32[128,256]{1,0:T(8,128)}, f32[128,256]{1,0:T(8,128)S(1)}, u32[]{:S(2)}, u32[]{:S(2)}) %collective-permute-start.1) | collective-permute-done | bytes 131104 | tf_op jit(solution)/shard_map/ppermute | solution.py:145
  12.6 0.7 %collective-permute-start.8 = (f32[128,256]{1,0:T(8,128)S(1)}, f32[128,256]{1,0:T(8,128)S(1)}, u32[]{:S(2)}, u32[]{:S(2)}) collective-permute-start(f32[128,256]{1,0:T(8,128)S(1)} %collective-permute-done.1.refs_2_), channel_id=1, source_target_pairs={{0,2},{1,3},{2,0},{3,1},{4,6},{5,7},{6,4},{7,5},{8,10},{9,11},{10,... | collective-permute-start | bytes 393224 | tf_op jit(solution)/shard_map/ppermute | solution.py:145
  13.3 0.0 collective-permute-done.3.refs_4_
  13.3 0.0 collective-permute-start.2
  13.3 0.0 collective-permute-done.refs_1_
  13.3 0.5 %collective-permute-start.4 = (f32[128,256]{1,0:T(8,128)S(1)}, f32[128,256]{1,0:T(8,128)S(1)}, u32[]{:S(2)}, u32[]{:S(2)}) collective-permute-start(f32[128,256]{1,0:T(8,128)S(1)} %collective-permute-done.3.refs_4_), channel_id=1, source_target_pairs={{0,1},{1,0},{2,3},{3,2},{4,5},{5,4},{6,7},{7,6},{8,9},{9,8},{10,11... | collective-permute-start | bytes 393224 | tf_op jit(solution)/shard_map/ppermute | solution.py:145
  13.8 3.8 %collective-permute-done.8.refs_5_ = f32[128,256]{1,0:T(8,128)S(1)} collective-permute-done((f32[128,256]{1,0:T(8,128)S(1)}, f32[128,256]{1,0:T(8,128)S(1)}, u32[]{:S(2)}, u32[]{:S(2)}) %collective-permute-start.8) | collective-permute-done | bytes 131104 | tf_op jit(solution)/shard_map/ppermute | solution.py:145
  17.6 0.0 collective-permute-start.9
  17.6 0.0 copy-start.2
  17.6 0.0 copy-start.3
  17.6 0.7 %copy-done.3 = s32[16]{0:T(128)S(1)} copy-done((s32[16]{0:T(128)S(1)}, s32[16]{0:T(128)}, u32[]{:S(2)}) %copy-start.3) | copy-done | bytes 88
  18.3 0.1 dynamic_slice.3
  18.4 0.0 collective-permute-done.2.refs_3_
  18.4 0.0 collective-permute-done.4.refs_5_
  18.4 0.0 collective-permute-done.6.refs_8_
  18.4 0.0 collective-permute-done.7.refs_9_
  18.4 0.0 copy-done.2
  18.4 0.0 copy-start
  18.4 0.9 %copy-done = f32[1,8,32,256]{3,2,1,0:T(8,128)S(1)} copy-done((f32[1,8,32,256]{3,2,1,0:T(8,128)S(1)}, f32[1,8,32,256]{3,2,1,0:T(8,128)}, u32[]{:S(2)}) %copy-start) | copy-done | bytes 262168
  19.3 0.0 copy-start.1
  19.3 0.9 %copy-done.1 = f32[256,4,1,32]{0,3,2,1:T(8,128)S(1)} copy-done((f32[256,4,1,32]{0,3,2,1:T(8,128)S(1)}, f32[256,4,1,32]{0,3,2,1:T(8,128)}, u32[]{:S(2)}) %copy-start.1) | copy-done | bytes 131096
  20.3 1.4 %shard_map.68 = (f32[256,256]{1,0:T(8,128)S(1)}, bf16[256,256]{1,0:T(8,128)(2,1)S(1)}, bf16[256,256]{1,0:T(8,128)(2,1)S(1)}, bf16[256,256]{1,0:T(8,128)(2,1)S(1)}, bf16[256,256]{1,0:T(8,128)(2,1)S(1)}) custom-call(f32[128,256]{1,0:T(8,128)S(1)} %bitcast.16, f32[128,256]{1,0:T(8,128)S(1)} %collective-permute-done.refs_1_, ...), custom_call_target="tpu_custom_call" | custom-call | flops 402653184 | bytes 8388608 | tf_op jit(solution)/shard_map/pallas_call | solution.py:174
  21.7 0.0 collective-permute-done.9.refs_6_
  21.7 0.0 copy-start.4
  21.7 1.7 %shard_map.69 = (f32[256,256]{1,0:T(8,128)}, f32[256,128]{1,0:T(8,128)S(1)}) custom-call(f32[256,256]{1,0:T(8,128)S(1)} %get-tuple-element.9.refs_0_, bf16[256,256]{1,0:T(8,128)(2,1)S(1)} %get-tuple-element.10.refs_1_, bf16[256,256]{1,0:T(8,128)(2,1)S(1)} %get-tuple-element.11.refs_2_, bf16[256,256]{1,0:T(8,128)(2,1)S(1)} %get-tuple-element.12.refs_3_, ...), custom_call_target="tpu_custom_call" | custom-call | tf_op jit(solution)/shard_map/pallas_call | solution.py:192
  23.4 1.4 %collective-permute-start.10 = (f32[256,128]{1,0:T(8,128)S(1)}, f32[256,128]{1,0:T(8,128)S(1)}, u32[]{:S(2)}, u32[]{:S(2)}) collective-permute-start(f32[256,128]{1,0:T(8,128)S(1)} %get-tuple-element.15), channel_id=1, source_target_pairs={{0,24},{1,25},{2,26},{3,27},{4,28},{5,29},{6,30},{7,31},{8,16},{9,... | collective-permute-start | bytes 393224 | tf_op jit(solution)/shard_map/ppermute | solution.py:145
  24.9 1.9 %collective-permute-start.11 = (f32[256,128]{1,0:T(8,128)S(1)}, f32[256,128]{1,0:T(8,128)S(1)}, u32[]{:S(2)}, u32[]{:S(2)}) collective-permute-start(f32[256,128]{1,0:T(8,128)S(1)} %get-tuple-element.15), channel_id=1, source_target_pairs={{0,16},{1,17},{2,18},{3,19},{4,20},{5,21},{6,22},{7,23},{8,24},{9,... | collective-permute-start | bytes 393224 | tf_op jit(solution)/shard_map/ppermute | solution.py:145
  26.8 0.1 collective-permute-start.12
  26.9 0.1 iota_compare_fusion
  27.0 3.7 %collective-permute-done.10 = f32[256,128]{1,0:T(8,128)S(1)} collective-permute-done((f32[256,128]{1,0:T(8,128)S(1)}, f32[256,128]{1,0:T(8,128)S(1)}, u32[]{:S(2)}, u32[]{:S(2)}) %collective-permute-start.10) | collective-permute-done | bytes 131104 | tf_op jit(solution)/shard_map/ppermute | solution.py:145
  30.7 2.4 %collective-permute-done.11 = f32[256,128]{1,0:T(8,128)S(1)} collective-permute-done((f32[256,128]{1,0:T(8,128)S(1)}, f32[256,128]{1,0:T(8,128)S(1)}, u32[]{:S(2)}, u32[]{:S(2)}) %collective-permute-start.11) | collective-permute-done | bytes 131104 | tf_op jit(solution)/shard_map/ppermute | solution.py:145
  33.1 0.0 collective-permute-done.12
  33.1 0.0 copy-done.4
  33.1 0.8 %subtract_select_fusion = f32[256,128]{1,0:T(8,128)} fusion(f32[256,128]{1,0:T(8,128)S(1)} %copy-done.4, f32[256,128]{1,0:T(8,128)S(1)} %collective-permute-done.12, f32[256,128]{1,0:T(8,128)S(1)} %collective-permute-done.11, f32[256,128]{1,0:T(8,128)S(1)} %get-tuple-element.15, f32[256,128]{1,0:T(8,128)S(1)} %collective-permute-done.10, ...), kind=kLoop, calls=%fused_computation | loop fusion | flops 196608 | bytes 786944 | tf_op jit(solution)/shard_map/jit(_where)/select_n | solution.py:214
Async XLA Ops:
  0.6 8.7 %collective-permute-start.5 = (f32[256,256]{1,0:T(8,128)}, f32[256,256]{1,0:T(8,128)S(1)}, u32[]{:S(2)}, u32[]{:S(2)}) collective-permute-start(f32[256,256]{1,0:T(8,128)} %bitcast.10), channel_id=1, source_target_pairs={{0,8},{1,17},{2,10},{3,19},{4,12},{5,21},{6,14},{7,23},{8,0},{9,25... | collective-permute-start | bytes 786440 | tf_op jit(solution)/shard_map/ppermute | solution.py:145
  3.6 9.0 %collective-permute-start.1 = (f32[128,256]{1,0:T(8,128)}, f32[128,256]{1,0:T(8,128)S(1)}, u32[]{:S(2)}, u32[]{:S(2)}) collective-permute-start(f32[128,256]{1,0:T(8,128)} %bitcast.13), channel_id=1, source_target_pairs={{0,4},{1,5},{2,6},{3,7},{4,0},{5,1},{6,2},{7,3},{8,12},{9,13},{10,... | collective-permute-start | bytes 393224 | tf_op jit(solution)/shard_map/ppermute | solution.py:145
  6.2 7.1 %collective-permute-start.3 = (f32[128,256]{1,0:T(8,128)}, f32[128,256]{1,0:T(8,128)S(1)}, u32[]{:S(2)}, u32[]{:S(2)}) collective-permute-start(f32[128,256]{1,0:T(8,128)} %bitcast.14), channel_id=1, source_target_pairs={{0,2},{1,3},{2,0},{3,1},{4,6},{5,7},{6,4},{7,5},{8,10},{9,11},{10,... | collective-permute-start | bytes 393224 | tf_op jit(solution)/shard_map/ppermute | solution.py:145
  7.8 5.5 %collective-permute-start = (f32[128,256]{1,0:T(8,128)}, f32[128,256]{1,0:T(8,128)S(1)}, u32[]{:S(2)}, u32[]{:S(2)}) collective-permute-start(f32[128,256]{1,0:T(8,128)} %bitcast.15), channel_id=1, source_target_pairs={{0,1},{1,0},{2,3},{3,2},{4,5},{5,4},{6,7},{7,6},{8,9},{9,8},{10,11... | collective-permute-start | bytes 393224 | tf_op jit(solution)/shard_map/ppermute | solution.py:145
  7.8 10.6 %collective-permute-start.6 = (f32[256,256]{1,0:T(8,128)}, f32[256,256]{1,0:T(8,128)S(1)}, u32[]{:S(2)}, u32[]{:S(2)}) collective-permute-start(f32[256,256]{1,0:T(8,128)} %bitcast.11), channel_id=1, source_target_pairs={{0,16},{1,9},{2,18},{3,11},{4,20},{5,13},{6,22},{7,15},{8,24},{9,1... | collective-permute-start | bytes 786440 | tf_op jit(solution)/shard_map/ppermute | solution.py:145
  9.3 9.0 %collective-permute-start.7 = (f32[256,256]{1,0:T(8,128)S(1)}, f32[256,256]{1,0:T(8,128)S(1)}, u32[]{:S(2)}, u32[]{:S(2)}) collective-permute-start(f32[256,256]{1,0:T(8,128)S(1)} %collective-permute-done.5.refs_7_), channel_id=1, source_target_pairs={{0,16},{1,9},{2,18},{3,11},{4,20},{5,13},{6,22},{7,15},{8,24},{9,1... | collective-permute-start | bytes 786440 | tf_op jit(solution)/shard_map/ppermute | solution.py:145
  12.6 5.0 %collective-permute-start.8 = (f32[128,256]{1,0:T(8,128)S(1)}, f32[128,256]{1,0:T(8,128)S(1)}, u32[]{:S(2)}, u32[]{:S(2)}) collective-permute-start(f32[128,256]{1,0:T(8,128)S(1)} %collective-permute-done.1.refs_2_), channel_id=1, source_target_pairs={{0,2},{1,3},{2,0},{3,1},{4,6},{5,7},{6,4},{7,5},{8,10},{9,11},{10,... | collective-permute-start | bytes 393224 | tf_op jit(solution)/shard_map/ppermute | solution.py:145
  13.3 5.0 %collective-permute-start.2 = (f32[128,256]{1,0:T(8,128)S(1)}, f32[128,256]{1,0:T(8,128)S(1)}, u32[]{:S(2)}, u32[]{:S(2)}) collective-permute-start(f32[128,256]{1,0:T(8,128)S(1)} %collective-permute-done.1.refs_2_), channel_id=1, source_target_pairs={{0,1},{1,0},{2,3},{3,2},{4,5},{5,4},{6,7},{7,6},{8,9},{9,8},{10,11... | collective-permute-start | bytes 393224 | tf_op jit(solution)/shard_map/ppermute | solution.py:145
  13.3 5.0 %collective-permute-start.4 = (f32[128,256]{1,0:T(8,128)S(1)}, f32[128,256]{1,0:T(8,128)S(1)}, u32[]{:S(2)}, u32[]{:S(2)}) collective-permute-start(f32[128,256]{1,0:T(8,128)S(1)} %collective-permute-done.3.refs_4_), channel_id=1, source_target_pairs={{0,1},{1,0},{2,3},{3,2},{4,5},{5,4},{6,7},{7,6},{8,9},{9,8},{10,11... | collective-permute-start | bytes 393224 | tf_op jit(solution)/shard_map/ppermute | solution.py:145
  17.6 4.1 %collective-permute-start.9 = (f32[128,256]{1,0:T(8,128)S(1)}, f32[128,256]{1,0:T(8,128)S(1)}, u32[]{:S(2)}, u32[]{:S(2)}) collective-permute-start(f32[128,256]{1,0:T(8,128)S(1)} %collective-permute-done.8.refs_5_), channel_id=1, source_target_pairs={{0,1},{1,0},{2,3},{3,2},{4,5},{5,4},{6,7},{7,6},{8,9},{9,8},{10,11... | collective-permute-start | bytes 393224 | tf_op jit(solution)/shard_map/ppermute | solution.py:145
  17.6 0.8 %copy-start.2 = (s32[8,16]{1,0:T(8,128)S(1)}, s32[8,16]{1,0:T(8,128)}, u32[]{:S(2)}) copy-start(s32[8,16]{1,0:T(8,128)} %refs_7_.1) | copy-start | bytes 1540
  17.6 0.7 %copy-start.3 = (s32[16]{0:T(128)S(1)}, s32[16]{0:T(128)}, u32[]{:S(2)}) copy-start(s32[16]{0:T(128)} %refs_8_.1) | copy-start | bytes 196
  18.4 1.0 %copy-start = (f32[1,8,32,256]{3,2,1,0:T(8,128)S(1)}, f32[1,8,32,256]{3,2,1,0:T(8,128)}, u32[]{:S(2)}) copy-start(f32[1,8,32,256]{3,2,1,0:T(8,128)} %param.6) | copy-start | bytes 786436
  19.3 0.9 %copy-start.1 = (f32[256,4,1,32]{0,3,2,1:T(8,128)S(1)}, f32[256,4,1,32]{0,3,2,1:T(8,128)}, u32[]{:S(2)}) copy-start(f32[256,4,1,32]{0,3,2,1:T(8,128)} %param.5) | copy-start | bytes 393220
  21.7 11.3 %copy-start.4 = (f32[256,128]{1,0:T(8,128)S(1)}, f32[256,128]{1,0:T(8,128)}, u32[]{:S(2)}) copy-start(f32[256,128]{1,0:T(8,128)} %param.7) | copy-start | bytes 393220
  23.4 7.2 %collective-permute-start.10 = (f32[256,128]{1,0:T(8,128)S(1)}, f32[256,128]{1,0:T(8,128)S(1)}, u32[]{:S(2)}, u32[]{:S(2)}) collective-permute-start(f32[256,128]{1,0:T(8,128)S(1)} %get-tuple-element.15), channel_id=1, source_target_pairs={{0,24},{1,25},{2,26},{3,27},{4,28},{5,29},{6,30},{7,31},{8,16},{9,... | collective-permute-start | bytes 393224 | tf_op jit(solution)/shard_map/ppermute | solution.py:145
  24.9 8.2 %collective-permute-start.11 = (f32[256,128]{1,0:T(8,128)S(1)}, f32[256,128]{1,0:T(8,128)S(1)}, u32[]{:S(2)}, u32[]{:S(2)}) collective-permute-start(f32[256,128]{1,0:T(8,128)S(1)} %get-tuple-element.15), channel_id=1, source_target_pairs={{0,16},{1,17},{2,18},{3,19},{4,20},{5,21},{6,22},{7,23},{8,24},{9,... | collective-permute-start | bytes 393224 | tf_op jit(solution)/shard_map/ppermute | solution.py:145
  26.8 6.3 %collective-permute-start.12 = (f32[256,128]{1,0:T(8,128)S(1)}, f32[256,128]{1,0:T(8,128)S(1)}, u32[]{:S(2)}, u32[]{:S(2)}) collective-permute-start(f32[256,128]{1,0:T(8,128)S(1)} %get-tuple-element.15), channel_id=1, source_target_pairs={{0,8},{1,9},{2,10},{3,11},{4,12},{5,13},{6,14},{7,15},{8,0},{9,1},... | collective-permute-start | bytes 393224 | tf_op jit(solution)/shard_map/ppermute | solution.py:145

commit v3 on v2

v3 whole, which is shorter than its diff:
```python
import functools
import jax
import jax.numpy as jnp
from jax import lax
from jax.experimental import pallas as pl
from jax.experimental.pallas import tpu as pltpu
from jax.sharding import PartitionSpec as P

ROW_STEP = 256


def offset_of(order, block):
    total = 0
    for place, bit in enumerate(order):
        if block >> place & 1:
            total ^= bit
    return total


def split(values):
    high = values.astype(jnp.bfloat16)
    return high, (values - high.astype(jnp.float32)).astype(jnp.bfloat16)


def dot3(a, b, dims):
    (a_high, a_low), (b_high, b_low) = a, b
    dot = functools.partial(
        lax.dot_general, dimension_numbers=(dims, ((), ())), preferred_element_type=jnp.float32
    )
    return dot(a_high, b_high) + (dot(a_high, b_low) + dot(a_low, b_high))


def rows_of_pair(ref, source, run, rows_here, row_count):
    pieces = []
    for column in (source, source ^ 1):
        for i in range(row_count):
            base = pl.multiple_of(i * rows_here + column * run, run)
            pieces.append(ref[pl.ds(base, run), :])
    return jnp.concatenate(pieces, axis=0)


def pair_product(lowers, own, other):
    panel = [jnp.concatenate(halves, axis=0) for halves in zip(own, other)]
    return dot3(lowers, panel, ((0,), (0,)))


def own_kernel(shape, lower_ref, panel_ref, pattern_ref, widths_ref, *refs):
    _, col_count, run, block_len, sup_here = shape
    lm_high, lm_low, panel_high, panel_low, row_mask, sel_mask, diag_mask, *refs = refs
    lower, panel, lower_sem, panel_sem = refs
    rows_here = col_count * run
    step = pl.program_id(0)
    rows = pl.ds(pl.multiple_of(step * ROW_STEP, ROW_STEP), ROW_STEP)
    lower_copy = pltpu.make_async_copy(lower_ref.at[rows, :], lower, lower_sem)
    panel_copy = pltpu.make_async_copy(panel_ref.at[:, rows], panel, panel_sem)
    lower_copy.start()
    panel_copy.start()
    sup = lax.axis_index("pcol") * sup_here
    first = lax.axis_index("prow") * (rows_here // block_len) + step * (ROW_STEP // block_len)
    square = (block_len, block_len)
    lanes = lax.broadcasted_iota(jnp.int32, square, 1)
    subs = lax.broadcasted_iota(jnp.int32, square, 0)
    line = lax.broadcasted_iota(jnp.int32, (1, block_len), 1)

    def ones_where(kept):
        return jnp.where(kept, 1.0, 0.0).astype(jnp.float32)

    for s in range(sup_here):
        cols = slice(s * block_len, (s + 1) * block_len)
        width = widths_ref[sup + s]
        diag_mask[cols, :] = ones_where((lanes < width) & (subs < width))
        for row_block in range(row_mask.shape[0]):
            kept = jnp.where(pattern_ref[row_block, sup + s] != 0, width, 0)
            row_mask[row_block : row_block + 1, cols] = ones_where(line < kept)
        for part in range(ROW_STEP // block_len):
            here = slice(part * block_len, (part + 1) * block_len)
            kept = jnp.where(pattern_ref[first + part, sup + s] != 0, width, 0)
            sel_mask[cols, here] = ones_where(subs < kept)
    lower_copy.wait()
    for part in range(ROW_STEP // block_len):
        here = slice(part * block_len, (part + 1) * block_len)
        mask = row_mask[pl.ds(first + part, 1), :]
        lm_high[here, :], lm_low[here, :] = split(lower[here, :] * mask)
    panel_copy.wait()
    panel_high[...], panel_low[...] = split(panel[...])


def early_kernel(shape, row_orders, col_offsets, *refs):
    row_count, col_count, run, block_len, sup_here = shape
    half = col_count // 2
    own_panel, refs = refs[:2], refs[2:]
    panel_refs, refs = refs[: 2 * half - 3], refs[2 * half - 3 :]
    own_lower, refs = refs[:2], refs[2:]
    lower_refs, refs = refs[: row_count - 1], refs[row_count - 1 :]
    row_mask, total_ref, lx_high, lx_low, lh, ll = refs
    row = lax.axis_index("prow")
    col = lax.axis_index("pcol")
    core = lax.rem(col, 2)
    rows_here = col_count * run

    @pl.when(pl.program_id(0) == 0)
    def _():
        mine = pl.ds(pl.multiple_of(row * rows_here, rows_here), rows_here)
        lh[mine, :] = own_lower[0][...]
        ll[mine, :] = own_lower[1][...]
        for block, ref in enumerate(lower_refs):
            first, second = (offset_of(order, block + 1) for order in row_orders)
            source = row ^ jnp.where(core == 0, first, second)
            for part in range(rows_here // block_len):
                row_block = source * (rows_here // block_len) + part
                base = pl.multiple_of(row_block * block_len, block_len)
                here = slice(part * block_len, (part + 1) * block_len)
                high, low = split(ref[here, :] * row_mask[pl.ds(row_block, 1), :])
                lh[pl.ds(base, block_len), :] = high
                ll[pl.ds(base, block_len), :] = low
        late = col ^ col_offsets[-1]
        lx_high[...] = rows_of_pair(lh, late, run, rows_here, row_count)
        lx_low[...] = rows_of_pair(ll, late, run, rows_here, row_count)

    total = None
    for block in range(half - 1):
        source = col ^ col_offsets[block]
        lowers = tuple(rows_of_pair(ref, source, run, rows_here, row_count) for ref in (lh, ll))
        if block == 0:
            own = tuple(ref[...] for ref in own_panel)
        else:
            own = split(panel_refs[2 * block - 1][...])
        part = pair_product(lowers, own, split(panel_refs[2 * block][...]))
        total = part if total is None else total + part
    total_ref[...] = total


def late_kernel(shape, *refs):
    _, _, _, block_len, sup_here = shape
    total_ref, lx_high, lx_low, lm_high, lm_low, own_ref, other_ref, mask_ref, *refs = refs
    chosen_ref, cross_ref = refs
    step = pl.program_id(0)
    lowers = (lx_high[...], lx_low[...])
    total = total_ref[...] + pair_product(lowers, split(own_ref[...]), split(other_ref[...]))
    chosen_all = -total * mask_ref[...]
    chosen_ref[...] = chosen_all
    for s in range(sup_here):
        cols = slice(s * block_len, (s + 1) * block_len)
        chosen = split(chosen_all[cols, :])
        crossed = dot3(chosen, (lm_high[:, cols], lm_low[:, cols]), ((1,), (0,)))

        @pl.when(step == 0)
        def _():
            cross_ref[cols, :] = crossed

        @pl.when(step != 0)
        def _():
            cross_ref[cols, :] += crossed


def store_kernel(chosen_ref, out_ref):
    out_ref[...] = chosen_ref[...]


def per_device(mesh_sizes, inverse_panel, lower_blocks, diag_inverse, pattern, widths):
    row_count, col_count = mesh_sizes
    rows_here, _, _, run = inverse_panel.shape
    width = lower_blocks.shape[3]
    block_len = diag_inverse.shape[1]
    sup_here = width // block_len
    half = col_count // 2
    depth = row_count * rows_here
    tall = row_count * run

    row_bits = [1 << b for b in range(row_count.bit_length() - 1)]
    col_bits = [1 << b for b in range(1, col_count.bit_length() - 1)][::-1]
    row_orders = (row_bits, row_bits[::-1])
    col_offsets = [offset_of(col_bits, block) for block in range(half)]

    def send(values, row_steps, col_step):
        pairs = []
        for r in range(row_count):
            for c in range(col_count):
                target = (r ^ row_steps[c % 2]) * col_count + (c ^ col_step)
                pairs.append((r * col_count + c, target))
        return lax.ppermute(values, ("prow", "pcol"), pairs)

    def along_rows(values, place):
        return send(values, [order[place] for order in row_orders], 0)

    def along_cols(values, place):
        return send(values, (0, 0), col_bits[place])

    def to_other_core(values):
        return send(values, (0, 0), 1)

    def after(values, *others):
        return lax.optimization_barrier((values, *others))[0]

    panel = jnp.transpose(inverse_panel, (1, 2, 3, 0)).reshape(tall, rows_here)
    lower = lower_blocks.reshape(rows_here, width)

    shape = (row_count, col_count, run, block_len, sup_here)
    grid = (rows_here // ROW_STEP,)
    panel_spec = pl.BlockSpec((tall, ROW_STEP), lambda i: (0, i))
    total_spec = pl.BlockSpec((width, ROW_STEP), lambda i: (0, i))
    lower_spec = pl.BlockSpec((ROW_STEP, width), lambda i: (i, 0))

    def fixed(*dims):
        return pl.BlockSpec(dims, lambda i: (0, 0), pipeline_mode=pl.Buffered(1))

    def out_fixed(*dims):
        return pl.BlockSpec(dims, lambda i: (0, 0))

    def array(rows, columns, dtype=jnp.float32):
        return jax.ShapeDtypeStruct((rows, columns), dtype)

    small = pltpu.CompilerParams(vmem_limit_bytes=12 << 20)
    smem = pl.BlockSpec(memory_space=pltpu.SMEM)
    in_hbm = pl.BlockSpec(memory_space=pltpu.HBM)
    row_blocks = depth // block_len
    *own_lower, own_high, own_low, row_mask, sel_mask, diag_mask = pl.pallas_call(
        functools.partial(own_kernel, shape),
        grid=grid,
        in_specs=[in_hbm, in_hbm, smem, smem],
        out_specs=[lower_spec] * 2
        + [panel_spec] * 2
        + [out_fixed(row_blocks, width), total_spec, out_fixed(width, block_len)],
        out_shape=[array(rows_here, width, jnp.bfloat16)] * 2
        + [array(tall, rows_here, jnp.bfloat16)] * 2
        + [array(row_blocks, width), array(width, rows_here), array(width, block_len)],
        scratch_shapes=[
            pltpu.VMEM((ROW_STEP, width), jnp.float32),
            pltpu.VMEM((tall, ROW_STEP), jnp.float32),
            pltpu.SemaphoreType.DMA,
            pltpu.SemaphoreType.DMA,
        ],
        compiler_params=small,
    )(lower, panel, pattern, widths)

    lowers = [lower]
    for place in range(len(row_bits)):
        lowers = lowers + [along_rows(values, place) for values in lowers]
    panels = [panel]
    for place in range(len(col_bits)):
        panels = panels + [along_cols(values, place) for values in panels]
    pairs = [v for values in panels[:-1] for v in (values, to_other_core(values))]

    early_bytes = 8 * depth * ROW_STEP + 8 * depth * width + 12 * rows_here * width
    total, *lower_parts = pl.pallas_call(
        functools.partial(early_kernel, shape, row_orders, col_offsets),
        grid=grid,
        in_specs=[panel_spec] * (2 * half - 1)
        + [fixed(rows_here, width)] * (row_count + 1)
        + [fixed(row_blocks, width)],
        out_specs=[total_spec, out_fixed(2 * tall, width), out_fixed(2 * tall, width)],
        out_shape=[array(width, rows_here)] + [array(2 * tall, width, jnp.bfloat16)] * 2,
        scratch_shapes=[pltpu.VMEM((depth, width), jnp.bfloat16)] * 2,
        compiler_params=pltpu.CompilerParams(vmem_limit_bytes=early_bytes + (6 << 20)),
        cost_estimate=pl.CostEstimate(
            flops=6 * depth * width * rows_here, bytes_accessed=8 << 20, transcendentals=0
        ),
    )(own_high, own_low, *pairs[1:], *own_lower, *lowers[1:], row_mask)
    last = after(panels[-1], total)
    chosen, crossed = pl.pallas_call(
        functools.partial(late_kernel, shape),
        grid=grid,
        in_specs=[total_spec, fixed(2 * tall, width), fixed(2 * tall, width)]
        + [lower_spec] * 2
        + [panel_spec, panel_spec, total_spec],
        out_specs=[total_spec, out_fixed(width, block_len)],
        out_shape=[array(width, rows_here), array(width, block_len)],
        compiler_params=small,
    )(total, *lower_parts, *own_lower, last, to_other_core(last), sel_mask)
    selected = pl.pallas_call(
        store_kernel,
        grid=grid,
        in_specs=[total_spec],
        out_specs=total_spec,
        out_shape=array(width, rows_here),
        compiler_params=small,
    )(chosen)

    arrived = [send(crossed, (block, block), 0) for block in range(1, row_count)][::-1]
    for values in arrived:
        crossed = crossed + values
    return selected, (diag_inverse - crossed) * diag_mask


def solution(mesh):
    placed = (
        P("prow", None, "pcol", None),
        P("prow", None, None, "pcol"),
        P("pcol", None),
        P(),
        P(),
    )
    return jax.shard_map(
        functools.partial(per_device, (mesh.shape["prow"], mesh.shape["pcol"])),
        mesh=mesh,
        in_specs=placed,
        out_specs=(P("pcol", "prow"), P("pcol", None)),
        check_vma=False,
    )
```

time: 34 us -> 31.2 us (0.918)
  waiting for transfers between devices: 12.2 us -> 8.95 us
  starting transfers between devices: 14.3 us -> 15 us
    ppermute x13, waiting for transfers between devices: 12.2 us -> 8.95 us  [send(): return lax.ppermute(values, ('prow', 'pcol'), pairs)]
    pallas_call x0 -> x2, Pallas kernels: none -> 1.64 us  [the longest x1 0.92 us: per_device(): pl.pallas_call(functools.partial(own_kernel, shape), grid=grid, in_specs=...]
    pallas_call x1, Pallas kernels: 1.7 us -> 0.63 us  [per_device(): pl.pallas_call(functools.partial(late_kernel, shape), grid=grid, in_specs...]
    select_n x1 -> x0, other arithmetic: 0.76 us -> none  [per_device(): diag_out = jnp.where(both_alive, difference, 0.0)]
    pallas_call x1, Pallas kernels: 1.45 us -> 0.7 us  [per_device(): pl.pallas_call(functools.partial(early_kernel, shape, row_orders, col_off...]
    mul x0 -> x1, other arithmetic: none -> 0.71 us  [per_device(): return (selected, (diag_inverse - crossed) * diag_mask)]
    ppermute x13, starting transfers between devices: 14.3 us -> 15 us  [send(): return lax.ppermute(values, ('prow', 'pcol'), pairs)]
  transfers between devices with their start and end apart: 13 -> 13, of which waited for: 4 -> 5; matrix products, arithmetic and copies ran while one was open for 0% -> 0% of each run, Pallas kernels for 4% -> 8%
where the time goes in v3:
time: 31.2 us; the launch traced here: 30.9 us
  starting transfers between devices  15 us (48%)
  waiting for transfers between devices  8.95 us (29%)
  Pallas kernels  2.97 us (10%)
  local copies, waits for them, and re-layouts  2.55 us (8%)
  between operations  0.72 us (2%)
  other arithmetic  0.71 us (2%)
    ppermute x13, starting transfers between devices, send(): return lax.ppermute(values, ('prow', 'pcol'), pairs)  15 us
    ppermute x13, waiting for transfers between devices, send(): return lax.ppermute(values, ('prow', 'pcol'), pairs)  8.95 us
    unnamed x10, local copies, waits for them, and re-layouts  2.55 us
    pallas_call x1, Pallas kernels, per_device(): pl.pallas_call(functools.partial(own_kernel, shape), grid=grid, in_specs=...  0.92 us
    pallas_call x1, Pallas kernels, per_device(): pl.pallas_call(store_kernel, grid=grid, in_specs=[total_spec], out_specs=...  0.72 us
    mul x1, other arithmetic, per_device(): return (selected, (diag_inverse - crossed) * diag_mask)  0.71 us
    pallas_call x1, Pallas kernels, per_device(): pl.pallas_call(functools.partial(early_kernel, shape, row_orders, col_off...  0.7 us
    pallas_call x1, Pallas kernels, per_device(): pl.pallas_call(functools.partial(late_kernel, shape), grid=grid, in_specs...  0.63 us
  transfers between devices with their start and end apart: 13, of which 5 were waited for; matrix products, arithmetic and copies ran while one was open for 0% of the time, Pallas kernels for 8%

profile of v3, /device:TPU:0, one launch (start us, length us, event | category | flops | bytes accessed | tf_op | source)
XLA Modules:
  0.0 30.9 jit_solution(11400557295704475070)
XLA Ops:
  0.6 0.0 copy-start.3
  0.6 3.0 %collective-permute-start.5 = (f32[256,256]{1,0:T(8,128)}, f32[256,256]{1,0:T(8,128)S(1)}, u32[]{:S(2)}, u32[]{:S(2)}) collective-permute-start(f32[256,256]{1,0:T(8,128)} %bitcast.4), channel_id=1, source_target_pairs={{0,8},{1,17},{2,10},{3,19},{4,12},{5,21},{6,14},{7,23},{8,0},{9,25... | collective-permute-start | bytes 786440 | tf_op jit(solution)/shard_map/ppermute | solution.py:181
  3.6 2.6 %collective-permute-start.1 = (f32[128,256]{1,0:T(8,128)}, f32[128,256]{1,0:T(8,128)S(1)}, u32[]{:S(2)}, u32[]{:S(2)}) collective-permute-start(f32[128,256]{1,0:T(8,128)} %bitcast.7), channel_id=1, source_target_pairs={{0,4},{1,5},{2,6},{3,7},{4,0},{5,1},{6,2},{7,3},{8,12},{9,13},{10,... | collective-permute-start | bytes 393224 | tf_op jit(solution)/shard_map/ppermute | solution.py:181
  6.2 1.6 %collective-permute-start.3 = (f32[128,256]{1,0:T(8,128)}, f32[128,256]{1,0:T(8,128)S(1)}, u32[]{:S(2)}, u32[]{:S(2)}) collective-permute-start(f32[128,256]{1,0:T(8,128)} %bitcast.8), channel_id=1, source_target_pairs={{0,2},{1,3},{2,0},{3,1},{4,6},{5,7},{6,4},{7,5},{8,10},{9,11},{10,... | collective-permute-start | bytes 393224 | tf_op jit(solution)/shard_map/ppermute | solution.py:181
  7.8 1.5 %collective-permute-start.6 = (f32[256,256]{1,0:T(8,128)}, f32[256,256]{1,0:T(8,128)S(1)}, u32[]{:S(2)}, u32[]{:S(2)}) collective-permute-start(f32[256,256]{1,0:T(8,128)} %bitcast.5), channel_id=1, source_target_pairs={{0,16},{1,9},{2,18},{3,11},{4,20},{5,13},{6,22},{7,15},{8,24},{9,1... | collective-permute-start | bytes 786440 | tf_op jit(solution)/shard_map/ppermute | solution.py:181
  9.3 0.0 collective-permute-done.5.refs_9_
  9.3 1.0 %collective-permute-start.7 = (f32[256,256]{1,0:T(8,128)S(1)}, f32[256,256]{1,0:T(8,128)S(1)}, u32[]{:S(2)}, u32[]{:S(2)}) collective-permute-start(f32[256,256]{1,0:T(8,128)S(1)} %collective-permute-done.5.refs_9_), channel_id=1, source_target_pairs={{0,16},{1,9},{2,18},{3,11},{4,20},{5,13},{6,22},{7,15},{8,24},{9,1... | collective-permute-start | bytes 786440 | tf_op jit(solution)/shard_map/ppermute | solution.py:181
  10.3 0.0 collective-permute-start
  10.3 2.3 %collective-permute-done.1.refs_3_ = f32[128,256]{1,0:T(8,128)S(1)} collective-permute-done((f32[128,256]{1,0:T(8,128)}, f32[128,256]{1,0:T(8,128)S(1)}, u32[]{:S(2)}, u32[]{:S(2)}) %collective-permute-start.1) | collective-permute-done | bytes 131104 | tf_op jit(solution)/shard_map/ppermute | solution.py:181
  12.7 0.0 collective-permute-start.2
  12.7 0.2 collective-permute-done.3.refs_5_
  12.9 0.3 collective-permute-start.4
  13.2 0.0 collective-permute-done.refs_2_
  13.2 1.4 %collective-permute-start.8 = (f32[128,256]{1,0:T(8,128)S(1)}, f32[128,256]{1,0:T(8,128)S(1)}, u32[]{:S(2)}, u32[]{:S(2)}) collective-permute-start(f32[128,256]{1,0:T(8,128)S(1)} %collective-permute-done.1.refs_3_), channel_id=1, source_target_pairs={{0,2},{1,3},{2,0},{3,1},{4,6},{5,7},{6,4},{7,5},{8,10},{9,11},{10,... | collective-permute-start | bytes 393224 | tf_op jit(solution)/shard_map/ppermute | solution.py:181
  14.6 0.0 copy-done.3
  14.6 0.0 copy-start
  14.6 0.9 %copy-done = f32[1,8,32,256]{3,2,1,0:T(8,128)S(1)} copy-done((f32[1,8,32,256]{3,2,1,0:T(8,128)S(1)}, f32[1,8,32,256]{3,2,1,0:T(8,128)}, u32[]{:S(2)}) %copy-start) | copy-done | bytes 262168
  15.5 0.0 copy-start.1
  15.5 0.9 %copy-done.1 = f32[256,4,1,32]{0,3,2,1:T(8,128)S(1)} copy-done((f32[256,4,1,32]{0,3,2,1:T(8,128)S(1)}, f32[256,4,1,32]{0,3,2,1:T(8,128)}, u32[]{:S(2)}) %copy-start.1) | copy-done | bytes 131096
  16.4 0.0 copy-start.2
  16.4 0.7 %copy-done.2 = s32[8,16]{1,0:T(8,128)S(1)} copy-done((s32[8,16]{1,0:T(8,128)S(1)}, s32[8,16]{1,0:T(8,128)}, u32[]{:S(2)}) %copy-start.2) | copy-done | bytes 536
  17.1 0.9 %shard_map.68 = (bf16[256,256]{1,0:T(8,128)(2,1)S(1)}, bf16[256,256]{1,0:T(8,128)(2,1)S(1)}, bf16[128,256]{1,0:T(8,128)(2,1)S(1)}, bf16[128,256]{1,0:T(8,128)(2,...) custom-call(f32[256,256]{1,0:T(8,128)S(1)} %bitcast.6, f32[128,256]{1,0:T(8,128)S(1)} %bitcast.10, ...), custom_call_target="tpu_custom_call" | custom-call | tf_op jit(solution)/shard_map/pallas_call | solution.py:217
  18.0 0.0 collective-permute-done.2.refs_4_
  18.0 0.0 collective-permute-done.4.refs_6_
  18.1 0.0 collective-permute-done.6.refs_10_
  18.1 0.0 collective-permute-done.7.refs_11_
  18.1 0.7 %shard_map.69 = (f32[256,256]{1,0:T(8,128)S(1)}, bf16[256,256]{1,0:T(8,128)(2,1)S(1)}, bf16[256,256]{1,0:T(8,128)(2,1)S(1)}) custom-call(bf16[128,256]{1,0:T(8,128)(2,1)S(1)} %get-tuple-element.15.refs_0_, bf16[128,256]{1,0:T(8,128)(2,1)S(1)} %get-tuple-element.16.refs_1_, f32[128,256]{1,0:T(8,128)S(1)} %collective-permute-done.refs_2_, ...), custom_call_target="tpu_custom_call" | custom-call | flops 402653184 | bytes 8388608 | tf_op jit(solution)/shard_map/pallas_call | solution.py:245
  18.8 0.0 collective-permute-done.8.refs_5_
  18.8 0.1 collective-permute-start.9
  18.9 1.3 %collective-permute-done.9.refs_6_ = f32[128,256]{1,0:T(8,128)S(1)} collective-permute-done((f32[128,256]{1,0:T(8,128)S(1)}, f32[128,256]{1,0:T(8,128)S(1)}, u32[]{:S(2)}, u32[]{:S(2)}) %collective-permute-start.9) | collective-permute-done | bytes 131104 | tf_op jit(solution)/shard_map/ppermute | solution.py:181
  20.2 0.6 %shard_map.70 = (f32[256,256]{1,0:T(8,128)S(1)}, f32[256,128]{1,0:T(8,128)S(1)}) custom-call(f32[256,256]{1,0:T(8,128)S(1)} %get-tuple-element.20.refs_0_, bf16[256,256]{1,0:T(8,128)(2,1)S(1)} %get-tuple-element.21.refs_1_, bf16[256,256]{1,0:T(8,128)(2,1)S(1)} %get-tuple-element.22.refs_2_, bf16[256,256]{1,0:T(8,128)(2,1)S(1)} %get-tuple-element.17.refs_7_.refs_3_, ...), custom_call_target="tpu_custom_call" | custom-call | tf_op jit(solution)/shard_map/pallas_call | solution.py:260
  20.9 1.4 %collective-permute-start.10 = (f32[256,128]{1,0:T(8,128)S(1)}, f32[256,128]{1,0:T(8,128)S(1)}, u32[]{:S(2)}, u32[]{:S(2)}) collective-permute-start(f32[256,128]{1,0:T(8,128)S(1)} %get-tuple-element.26), channel_id=1, source_target_pairs={{0,24},{1,25},{2,26},{3,27},{4,28},{5,29},{6,30},{7,31},{8,16},{9,... | collective-permute-start | bytes 393224 | tf_op jit(solution)/shard_map/ppermute | solution.py:181
  22.3 1.6 %collective-permute-start.11 = (f32[256,128]{1,0:T(8,128)S(1)}, f32[256,128]{1,0:T(8,128)S(1)}, u32[]{:S(2)}, u32[]{:S(2)}) collective-permute-start(f32[256,128]{1,0:T(8,128)S(1)} %get-tuple-element.26), channel_id=1, source_target_pairs={{0,16},{1,17},{2,18},{3,19},{4,20},{5,21},{6,22},{7,23},{8,24},{9,... | collective-permute-start | bytes 393224 | tf_op jit(solution)/shard_map/ppermute | solution.py:181
  23.9 0.5 %collective-permute-start.12 = (f32[256,128]{1,0:T(8,128)S(1)}, f32[256,128]{1,0:T(8,128)S(1)}, u32[]{:S(2)}, u32[]{:S(2)}) collective-permute-start(f32[256,128]{1,0:T(8,128)S(1)} %get-tuple-element.26), channel_id=1, source_target_pairs={{0,8},{1,9},{2,10},{3,11},{4,12},{5,13},{6,14},{7,15},{8,0},{9,1},... | collective-permute-start | bytes 393224 | tf_op jit(solution)/shard_map/ppermute | solution.py:181
  24.4 0.0 copy-start.4
  24.4 0.7 %shard_map.71 = f32[256,256]{1,0:T(8,128)} custom-call(f32[256,256]{1,0:T(8,128)S(1)} %get-tuple-element.25.chosen_ref), custom_call_target="tpu_custom_call" | custom-call | tf_op jit(solution)/shard_map/pallas_call | solution.py:270
  25.1 3.1 %collective-permute-done.10 = f32[256,128]{1,0:T(8,128)S(1)} collective-permute-done((f32[256,128]{1,0:T(8,128)S(1)}, f32[256,128]{1,0:T(8,128)S(1)}, u32[]{:S(2)}, u32[]{:S(2)}) %collective-permute-start.10) | collective-permute-done | bytes 131104 | tf_op jit(solution)/shard_map/ppermute | solution.py:181
  28.2 2.0 %collective-permute-done.11 = f32[256,128]{1,0:T(8,128)S(1)} collective-permute-done((f32[256,128]{1,0:T(8,128)S(1)}, f32[256,128]{1,0:T(8,128)S(1)}, u32[]{:S(2)}, u32[]{:S(2)}) %collective-permute-start.11) | collective-permute-done | bytes 131104 | tf_op jit(solution)/shard_map/ppermute | solution.py:181
  30.2 0.0 collective-permute-done.12
  30.2 0.0 copy-done.4
  30.2 0.7 %subtract_multiply_fusion = f32[256,128]{1,0:T(8,128)} fusion(f32[256,128]{1,0:T(8,128)S(1)} %get-tuple-element.27, f32[256,128]{1,0:T(8,128)S(1)} %copy-done.4, f32[256,128]{1,0:T(8,128)S(1)} %collective-permute-done.12, f32[256,128]{1,0:T(8,128)S(1)} %collective-permute-done.11, f32[256,128]{1,0:T(8,128)S(1)} %get-tuple-element.26, ...), kind=kLoop, calls=%fused_computation | loop fusion | flops 163840 | bytes 917504 | tf_op jit(solution)/shard_map/mul | solution.py:282
Async XLA Ops:
  0.6 13.9 %copy-start.3 = (s32[16]{0:T(128)S(1)}, s32[16]{0:T(128)}, u32[]{:S(2)}) copy-start(s32[16]{0:T(128)} %widths_ref.1) | copy-start | bytes 196
  0.6 8.7 %collective-permute-start.5 = (f32[256,256]{1,0:T(8,128)}, f32[256,256]{1,0:T(8,128)S(1)}, u32[]{:S(2)}, u32[]{:S(2)}) collective-permute-start(f32[256,256]{1,0:T(8,128)} %bitcast.4), channel_id=1, source_target_pairs={{0,8},{1,17},{2,10},{3,19},{4,12},{5,21},{6,14},{7,23},{8,0},{9,25... | collective-permute-start | bytes 786440 | tf_op jit(solution)/shard_map/ppermute | solution.py:181
  3.6 9.0 %collective-permute-start.1 = (f32[128,256]{1,0:T(8,128)}, f32[128,256]{1,0:T(8,128)S(1)}, u32[]{:S(2)}, u32[]{:S(2)}) collective-permute-start(f32[128,256]{1,0:T(8,128)} %bitcast.7), channel_id=1, source_target_pairs={{0,4},{1,5},{2,6},{3,7},{4,0},{5,1},{6,2},{7,3},{8,12},{9,13},{10,... | collective-permute-start | bytes 393224 | tf_op jit(solution)/shard_map/ppermute | solution.py:181
  6.2 6.6 %collective-permute-start.3 = (f32[128,256]{1,0:T(8,128)}, f32[128,256]{1,0:T(8,128)S(1)}, u32[]{:S(2)}, u32[]{:S(2)}) collective-permute-start(f32[128,256]{1,0:T(8,128)} %bitcast.8), channel_id=1, source_target_pairs={{0,2},{1,3},{2,0},{3,1},{4,6},{5,7},{6,4},{7,5},{8,10},{9,11},{10,... | collective-permute-start | bytes 393224 | tf_op jit(solution)/shard_map/ppermute | solution.py:181
  7.8 10.2 %collective-permute-start.6 = (f32[256,256]{1,0:T(8,128)}, f32[256,256]{1,0:T(8,128)S(1)}, u32[]{:S(2)}, u32[]{:S(2)}) collective-permute-start(f32[256,256]{1,0:T(8,128)} %bitcast.5), channel_id=1, source_target_pairs={{0,16},{1,9},{2,18},{3,11},{4,20},{5,13},{6,22},{7,15},{8,24},{9,1... | collective-permute-start | bytes 786440 | tf_op jit(solution)/shard_map/ppermute | solution.py:181
  9.3 8.7 %collective-permute-start.7 = (f32[256,256]{1,0:T(8,128)S(1)}, f32[256,256]{1,0:T(8,128)S(1)}, u32[]{:S(2)}, u32[]{:S(2)}) collective-permute-start(f32[256,256]{1,0:T(8,128)S(1)} %collective-permute-done.5.refs_9_), channel_id=1, source_target_pairs={{0,16},{1,9},{2,18},{3,11},{4,20},{5,13},{6,22},{7,15},{8,24},{9,1... | collective-permute-start | bytes 786440 | tf_op jit(solution)/shard_map/ppermute | solution.py:181
  10.3 2.9 %collective-permute-start = (f32[128,256]{1,0:T(8,128)}, f32[128,256]{1,0:T(8,128)S(1)}, u32[]{:S(2)}, u32[]{:S(2)}) collective-permute-start(f32[128,256]{1,0:T(8,128)} %bitcast.9), channel_id=1, source_target_pairs={{0,1},{1,0},{2,3},{3,2},{4,5},{5,4},{6,7},{7,6},{8,9},{9,8},{10,11... | collective-permute-start | bytes 393224 | tf_op jit(solution)/shard_map/ppermute | solution.py:181
  12.7 5.4 %collective-permute-start.2 = (f32[128,256]{1,0:T(8,128)S(1)}, f32[128,256]{1,0:T(8,128)S(1)}, u32[]{:S(2)}, u32[]{:S(2)}) collective-permute-start(f32[128,256]{1,0:T(8,128)S(1)} %collective-permute-done.1.refs_3_), channel_id=1, source_target_pairs={{0,1},{1,0},{2,3},{3,2},{4,5},{5,4},{6,7},{7,6},{8,9},{9,8},{10,11... | collective-permute-start | bytes 393224 | tf_op jit(solution)/shard_map/ppermute | solution.py:181
  12.9 5.2 %collective-permute-start.4 = (f32[128,256]{1,0:T(8,128)S(1)}, f32[128,256]{1,0:T(8,128)S(1)}, u32[]{:S(2)}, u32[]{:S(2)}) collective-permute-start(f32[128,256]{1,0:T(8,128)S(1)} %collective-permute-done.3.refs_5_), channel_id=1, source_target_pairs={{0,1},{1,0},{2,3},{3,2},{4,5},{5,4},{6,7},{7,6},{8,9},{9,8},{10,11... | collective-permute-start | bytes 393224 | tf_op jit(solution)/shard_map/ppermute | solution.py:181
  13.2 5.6 %collective-permute-start.8 = (f32[128,256]{1,0:T(8,128)S(1)}, f32[128,256]{1,0:T(8,128)S(1)}, u32[]{:S(2)}, u32[]{:S(2)}) collective-permute-start(f32[128,256]{1,0:T(8,128)S(1)} %collective-permute-done.1.refs_3_), channel_id=1, source_target_pairs={{0,2},{1,3},{2,0},{3,1},{4,6},{5,7},{6,4},{7,5},{8,10},{9,11},{10,... | collective-permute-start | bytes 393224 | tf_op jit(solution)/shard_map/ppermute | solution.py:181
  14.6 1.0 %copy-start = (f32[1,8,32,256]{3,2,1,0:T(8,128)S(1)}, f32[1,8,32,256]{3,2,1,0:T(8,128)}, u32[]{:S(2)}) copy-start(f32[1,8,32,256]{3,2,1,0:T(8,128)} %param.6) | copy-start | bytes 786436
  15.5 0.9 %copy-start.1 = (f32[256,4,1,32]{0,3,2,1:T(8,128)S(1)}, f32[256,4,1,32]{0,3,2,1:T(8,128)}, u32[]{:S(2)}) copy-start(f32[256,4,1,32]{0,3,2,1:T(8,128)} %param.5) | copy-start | bytes 393220
  16.4 0.7 %copy-start.2 = (s32[8,16]{1,0:T(8,128)S(1)}, s32[8,16]{1,0:T(8,128)}, u32[]{:S(2)}) copy-start(s32[8,16]{1,0:T(8,128)} %pattern_ref.1) | copy-start | bytes 1540
  18.8 1.4 %collective-permute-start.9 = (f32[128,256]{1,0:T(8,128)S(1)}, f32[128,256]{1,0:T(8,128)S(1)}, u32[]{:S(2)}, u32[]{:S(2)}) collective-permute-start(f32[128,256]{1,0:T(8,128)S(1)} %collective-permute-done.8.refs_5_), channel_id=1, source_target_pairs={{0,1},{1,0},{2,3},{3,2},{4,5},{5,4},{6,7},{7,6},{8,9},{9,8},{10,11... | collective-permute-start | bytes 393224 | tf_op jit(solution)/shard_map/ppermute | solution.py:181
  20.9 7.3 %collective-permute-start.10 = (f32[256,128]{1,0:T(8,128)S(1)}, f32[256,128]{1,0:T(8,128)S(1)}, u32[]{:S(2)}, u32[]{:S(2)}) collective-permute-start(f32[256,128]{1,0:T(8,128)S(1)} %get-tuple-element.26), channel_id=1, source_target_pairs={{0,24},{1,25},{2,26},{3,27},{4,28},{5,29},{6,30},{7,31},{8,16},{9,... | collective-permute-start | bytes 393224 | tf_op jit(solution)/shard_map/ppermute | solution.py:181
  22.3 7.9 %collective-permute-start.11 = (f32[256,128]{1,0:T(8,128)S(1)}, f32[256,128]{1,0:T(8,128)S(1)}, u32[]{:S(2)}, u32[]{:S(2)}) collective-permute-start(f32[256,128]{1,0:T(8,128)S(1)} %get-tuple-element.26), channel_id=1, source_target_pairs={{0,16},{1,17},{2,18},{3,19},{4,20},{5,21},{6,22},{7,23},{8,24},{9,... | collective-permute-start | bytes 393224 | tf_op jit(solution)/shard_map/ppermute | solution.py:181
  23.9 6.3 %collective-permute-start.12 = (f32[256,128]{1,0:T(8,128)S(1)}, f32[256,128]{1,0:T(8,128)S(1)}, u32[]{:S(2)}, u32[]{:S(2)}) collective-permute-start(f32[256,128]{1,0:T(8,128)S(1)} %get-tuple-element.26), channel_id=1, source_target_pairs={{0,8},{1,9},{2,10},{3,11},{4,12},{5,13},{6,14},{7,15},{8,0},{9,1},... | collective-permute-start | bytes 393224 | tf_op jit(solution)/shard_map/ppermute | solution.py:181
  24.4 5.8 %copy-start.4 = (f32[256,128]{1,0:T(8,128)S(1)}, f32[256,128]{1,0:T(8,128)}, u32[]{:S(2)}) copy-start(f32[256,128]{1,0:T(8,128)} %param.7) | copy-start | bytes 393220

commit v4 on v3

--- a/solution.py
+++ b/solution.py
@@ -231,7 +231,7 @@
             pltpu.SemaphoreType.DMA,
         ],
         compiler_params=small,
-    )(lower, panel, pattern, widths)
+    )(*(pltpu.with_memory_space_constraint(v, pltpu.HBM) for v in (lower, panel, pattern, widths)))
 
     lowers = [lower]
     for place in range(len(row_bits)):
@@ -239,7 +239,9 @@
     panels = [panel]
     for place in range(len(col_bits)):
         panels = panels + [along_cols(values, place) for values in panels]
-    pairs = [v for values in panels[:-1] for v in (values, to_other_core(values))]
+    pairs = [panel, to_other_core(panel)]
+    for values in panels[1:-1]:
+        pairs += [values, to_other_core(after(values, own_high))]
 
     early_bytes = 8 * depth * ROW_STEP + 8 * depth * width + 12 * rows_here * width
     total, *lower_parts = pl.pallas_call(
@@ -256,7 +258,7 @@
             flops=6 * depth * width * rows_here, bytes_accessed=8 << 20, transcendentals=0
         ),
     )(own_high, own_low, *pairs[1:], *own_lower, *lowers[1:], row_mask)
-    last = after(panels[-1], total)
+    last = panels[-1]
     chosen, crossed = pl.pallas_call(
         functools.partial(late_kernel, shape),
         grid=grid,

time: 31.2 us -> 29.8 us (0.955)
  local copies, waits for them, and re-layouts: 2.55 us -> 0.01 us
  waiting for transfers between devices: 8.95 us -> 10 us
  Pallas kernels: 2.97 us -> 3.82 us
  starting transfers between devices: 15 us -> 14.4 us
    unnamed x10 -> x2, local copies, waits for them, and re-layouts: 2.55 us -> 0.01 us
    ppermute x13, waiting for transfers between devices: 8.95 us -> 10 us  [send(): return lax.ppermute(values, ('prow', 'pcol'), pairs)]
    pallas_call x1, Pallas kernels: 0.92 us -> 1.76 us  [per_device(): pl.pallas_call(functools.partial(own_kernel, shape), grid=grid, in_specs=...]
    ppermute x13, starting transfers between devices: 15 us -> 14.4 us  [send(): return lax.ppermute(values, ('prow', 'pcol'), pairs)]
  transfers between devices with their start and end apart: 13 -> 13, of which waited for: 5 -> 5; matrix products, arithmetic and copies ran while one was open for 0% -> 0% of each run, Pallas kernels for 8% -> 11%
where the time goes in v4:
time: 29.8 us; the launch traced here: 29.6 us
  starting transfers between devices  14.4 us (48%)
  waiting for transfers between devices  10 us (34%)
  Pallas kernels  3.82 us (13%)
  other arithmetic  0.71 us (2%)
  between operations  0.71 us (2%)
    ppermute x13, starting transfers between devices, send(): return lax.ppermute(values, ('prow', 'pcol'), pairs)  14.4 us
    ppermute x13, waiting for transfers between devices, send(): return lax.ppermute(values, ('prow', 'pcol'), pairs)  10 us
    pallas_call x1, Pallas kernels, per_device(): pl.pallas_call(functools.partial(own_kernel, shape), grid=grid, in_specs=...  1.76 us
    pallas_call x1, Pallas kernels, per_device(): pl.pallas_call(store_kernel, grid=grid, in_specs=[total_spec], out_specs=...  0.72 us
    mul x1, other arithmetic, per_device(): return (selected, (diag_inverse - crossed) * diag_mask)  0.71 us
    pallas_call x1, Pallas kernels, per_device(): pl.pallas_call(functools.partial(early_kernel, shape, row_orders, col_off...  0.71 us
    pallas_call x1, Pallas kernels, per_device(): pl.pallas_call(functools.partial(late_kernel, shape), grid=grid, in_specs...  0.63 us
  transfers between devices with their start and end apart: 13, of which 5 were waited for; matrix products, arithmetic and copies ran while one was open for 0% of the time, Pallas kernels for 11%

profile of v4, /device:TPU:0, one launch (start us, length us, event | category | flops | bytes accessed | tf_op | source)
XLA Modules:
  0.0 29.6 jit_solution(5961270541527408200)
XLA Ops:
  0.6 3.0 %collective-permute-start.5 = (f32[256,256]{1,0:T(8,128)}, f32[256,256]{1,0:T(8,128)S(1)}, u32[]{:S(2)}, u32[]{:S(2)}) collective-permute-start(f32[256,256]{1,0:T(8,128)} %bitcast.4), channel_id=1, source_target_pairs={{0,8},{1,17},{2,10},{3,19},{4,12},{5,21},{6,14},{7,23},{8,0},{9,25... | collective-permute-start | bytes 786440 | tf_op jit(solution)/shard_map/ppermute | solution.py:181
  3.6 2.6 %collective-permute-start.1 = (f32[128,256]{1,0:T(8,128)}, f32[128,256]{1,0:T(8,128)S(1)}, u32[]{:S(2)}, u32[]{:S(2)}) collective-permute-start(f32[128,256]{1,0:T(8,128)} %bitcast.7), channel_id=1, source_target_pairs={{0,4},{1,5},{2,6},{3,7},{4,0},{5,1},{6,2},{7,3},{8,12},{9,13},{10,... | collective-permute-start | bytes 393224 | tf_op jit(solution)/shard_map/ppermute | solution.py:181
  6.2 1.6 %collective-permute-start.3 = (f32[128,256]{1,0:T(8,128)}, f32[128,256]{1,0:T(8,128)S(1)}, u32[]{:S(2)}, u32[]{:S(2)}) collective-permute-start(f32[128,256]{1,0:T(8,128)} %bitcast.8), channel_id=1, source_target_pairs={{0,2},{1,3},{2,0},{3,1},{4,6},{5,7},{6,4},{7,5},{8,10},{9,11},{10,... | collective-permute-start | bytes 393224 | tf_op jit(solution)/shard_map/ppermute | solution.py:181
  7.8 0.0 collective-permute-start
  7.8 1.5 %collective-permute-start.6 = (f32[256,256]{1,0:T(8,128)}, f32[256,256]{1,0:T(8,128)S(1)}, u32[]{:S(2)}, u32[]{:S(2)}) collective-permute-start(f32[256,256]{1,0:T(8,128)} %bitcast.5), channel_id=1, source_target_pairs={{0,16},{1,9},{2,18},{3,11},{4,20},{5,13},{6,22},{7,15},{8,24},{9,1... | collective-permute-start | bytes 786440 | tf_op jit(solution)/shard_map/ppermute | solution.py:181
  9.3 0.0 collective-permute-done.5.refs_9_
  9.3 0.9 %collective-permute-start.7 = (f32[256,256]{1,0:T(8,128)S(1)}, f32[256,256]{1,0:T(8,128)S(1)}, u32[]{:S(2)}, u32[]{:S(2)}) collective-permute-start(f32[256,256]{1,0:T(8,128)S(1)} %collective-permute-done.5.refs_9_), channel_id=1, source_target_pairs={{0,16},{1,9},{2,18},{3,11},{4,20},{5,13},{6,22},{7,15},{8,24},{9,1... | collective-permute-start | bytes 786440 | tf_op jit(solution)/shard_map/ppermute | solution.py:181
  10.2 2.4 %collective-permute-done.1.refs_3_ = f32[128,256]{1,0:T(8,128)S(1)} collective-permute-done((f32[128,256]{1,0:T(8,128)}, f32[128,256]{1,0:T(8,128)S(1)}, u32[]{:S(2)}, u32[]{:S(2)}) %collective-permute-start.1) | collective-permute-done | bytes 131104 | tf_op jit(solution)/shard_map/ppermute | solution.py:181
  12.6 0.7 %collective-permute-start.8 = (f32[128,256]{1,0:T(8,128)S(1)}, f32[128,256]{1,0:T(8,128)S(1)}, u32[]{:S(2)}, u32[]{:S(2)}) collective-permute-start(f32[128,256]{1,0:T(8,128)S(1)} %collective-permute-done.1.refs_3_), channel_id=1, source_target_pairs={{0,2},{1,3},{2,0},{3,1},{4,6},{5,7},{6,4},{7,5},{8,10},{9,11},{10,... | collective-permute-start | bytes 393224 | tf_op jit(solution)/shard_map/ppermute | solution.py:181
  13.3 1.8 %shard_map.68 = (bf16[256,256]{1,0:T(8,128)(2,1)S(1)}, bf16[256,256]{1,0:T(8,128)(2,1)S(1)}, bf16[128,256]{1,0:T(8,128)(2,1)S(1)}, bf16[128,256]{1,0:T(8,128)(2,...) custom-call(f32[256,256]{1,0:T(8,128)} %bitcast.6, f32[128,256]{1,0:T(8,128)} %bitcast.10, ...), custom_call_target="tpu_custom_call" | custom-call | tf_op jit(solution)/shard_map/pallas_call | solution.py:217
  15.1 0.0 collective-permute-done.3.refs_5_
  15.1 0.1 collective-permute-start.2
  15.2 0.0 collective-permute-done.refs_2_
  15.2 0.5 %collective-permute-start.4 = (f32[128,256]{1,0:T(8,128)S(1)}, f32[128,256]{1,0:T(8,128)S(1)}, u32[]{:S(2)}, u32[]{:S(2)}) collective-permute-start(f32[128,256]{1,0:T(8,128)S(1)} %collective-permute-done.3.refs_5_), channel_id=1, source_target_pairs={{0,1},{1,0},{2,3},{3,2},{4,5},{5,4},{6,7},{7,6},{8,9},{9,8},{10,11... | collective-permute-start | bytes 393224 | tf_op jit(solution)/shard_map/ppermute | solution.py:181
  15.7 1.9 %collective-permute-done.8.refs_5_ = f32[128,256]{1,0:T(8,128)S(1)} collective-permute-done((f32[128,256]{1,0:T(8,128)S(1)}, f32[128,256]{1,0:T(8,128)S(1)}, u32[]{:S(2)}, u32[]{:S(2)}) %collective-permute-start.8) | collective-permute-done | bytes 131104 | tf_op jit(solution)/shard_map/ppermute | solution.py:181
  17.6 0.0 collective-permute-start.9
  17.6 0.0 collective-permute-done.2.refs_4_
  17.6 0.0 collective-permute-done.4.refs_6_
  17.6 0.0 collective-permute-done.6.refs_10_
  17.6 0.0 collective-permute-done.7.refs_11_
  17.6 0.7 %shard_map.69 = (f32[256,256]{1,0:T(8,128)S(1)}, bf16[256,256]{1,0:T(8,128)(2,1)S(1)}, bf16[256,256]{1,0:T(8,128)(2,1)S(1)}) custom-call(bf16[128,256]{1,0:T(8,128)(2,1)S(1)} %get-tuple-element.16.refs_0_, bf16[128,256]{1,0:T(8,128)(2,1)S(1)} %get-tuple-element.17.refs_1_, f32[128,256]{1,0:T(8,128)S(1)} %collective-permute-done.refs_2_, ...), custom_call_target="tpu_custom_call" | custom-call | flops 402653184 | bytes 8388608 | tf_op jit(solution)/shard_map/pallas_call | solution.py:247
  18.4 0.6 %collective-permute-done.9.refs_6_ = f32[128,256]{1,0:T(8,128)S(1)} collective-permute-done((f32[128,256]{1,0:T(8,128)S(1)}, f32[128,256]{1,0:T(8,128)S(1)}, u32[]{:S(2)}, u32[]{:S(2)}) %collective-permute-start.9) | collective-permute-done | bytes 131104 | tf_op jit(solution)/shard_map/ppermute | solution.py:181
  19.0 0.6 %shard_map.70 = (f32[256,256]{1,0:T(8,128)S(1)}, f32[256,128]{1,0:T(8,128)S(1)}) custom-call(f32[256,256]{1,0:T(8,128)S(1)} %get-tuple-element.23.refs_0_, bf16[256,256]{1,0:T(8,128)(2,1)S(1)} %get-tuple-element.24.refs_1_, bf16[256,256]{1,0:T(8,128)(2,1)S(1)} %get-tuple-element.25.refs_2_, bf16[256,256]{1,0:T(8,128)(2,1)S(1)} %get-tuple-element.20.refs_7_.refs_3_, ...), custom_call_target="tpu_custom_call" | custom-call | tf_op jit(solution)/shard_map/pallas_call | solution.py:262
  19.6 1.5 %collective-permute-start.10 = (f32[256,128]{1,0:T(8,128)S(1)}, f32[256,128]{1,0:T(8,128)S(1)}, u32[]{:S(2)}, u32[]{:S(2)}) collective-permute-start(f32[256,128]{1,0:T(8,128)S(1)} %get-tuple-element.28), channel_id=1, source_target_pairs={{0,24},{1,25},{2,26},{3,27},{4,28},{5,29},{6,30},{7,31},{8,16},{9,... | collective-permute-start | bytes 393224 | tf_op jit(solution)/shard_map/ppermute | solution.py:181
  21.1 1.9 %collective-permute-start.11 = (f32[256,128]{1,0:T(8,128)S(1)}, f32[256,128]{1,0:T(8,128)S(1)}, u32[]{:S(2)}, u32[]{:S(2)}) collective-permute-start(f32[256,128]{1,0:T(8,128)S(1)} %get-tuple-element.28), channel_id=1, source_target_pairs={{0,16},{1,17},{2,18},{3,19},{4,20},{5,21},{6,22},{7,23},{8,24},{9,... | collective-permute-start | bytes 393224 | tf_op jit(solution)/shard_map/ppermute | solution.py:181
  23.0 0.1 collective-permute-start.12
  23.2 0.0 copy-start
  23.2 0.7 %shard_map.71 = f32[256,256]{1,0:T(8,128)} custom-call(f32[256,256]{1,0:T(8,128)S(1)} %get-tuple-element.27.chosen_ref), custom_call_target="tpu_custom_call" | custom-call | tf_op jit(solution)/shard_map/pallas_call | solution.py:272
  23.9 3.0 %collective-permute-done.10 = f32[256,128]{1,0:T(8,128)S(1)} collective-permute-done((f32[256,128]{1,0:T(8,128)S(1)}, f32[256,128]{1,0:T(8,128)S(1)}, u32[]{:S(2)}, u32[]{:S(2)}) %collective-permute-start.10) | collective-permute-done | bytes 131104 | tf_op jit(solution)/shard_map/ppermute | solution.py:181
  26.9 2.0 %collective-permute-done.11 = f32[256,128]{1,0:T(8,128)S(1)} collective-permute-done((f32[256,128]{1,0:T(8,128)S(1)}, f32[256,128]{1,0:T(8,128)S(1)}, u32[]{:S(2)}, u32[]{:S(2)}) %collective-permute-start.11) | collective-permute-done | bytes 131104 | tf_op jit(solution)/shard_map/ppermute | solution.py:181
  28.9 0.0 collective-permute-done.12
  28.9 0.0 copy-done
  28.9 0.7 %subtract_multiply_fusion = f32[256,128]{1,0:T(8,128)} fusion(f32[256,128]{1,0:T(8,128)S(1)} %get-tuple-element.29, f32[256,128]{1,0:T(8,128)S(1)} %copy-done, f32[256,128]{1,0:T(8,128)S(1)} %collective-permute-done.12, f32[256,128]{1,0:T(8,128)S(1)} %collective-permute-done.11, f32[256,128]{1,0:T(8,128)S(1)} %get-tuple-element.28, ...), kind=kLoop, calls=%fused_computation | loop fusion | flops 163840 | bytes 917504 | tf_op jit(solution)/shard_map/mul | solution.py:284
Async XLA Ops:
  0.6 8.7 %collective-permute-start.5 = (f32[256,256]{1,0:T(8,128)}, f32[256,256]{1,0:T(8,128)S(1)}, u32[]{:S(2)}, u32[]{:S(2)}) collective-permute-start(f32[256,256]{1,0:T(8,128)} %bitcast.4), channel_id=1, source_target_pairs={{0,8},{1,17},{2,10},{3,19},{4,12},{5,21},{6,14},{7,23},{8,0},{9,25... | collective-permute-start | bytes 786440 | tf_op jit(solution)/shard_map/ppermute | solution.py:181
  3.6 9.0 %collective-permute-start.1 = (f32[128,256]{1,0:T(8,128)}, f32[128,256]{1,0:T(8,128)S(1)}, u32[]{:S(2)}, u32[]{:S(2)}) collective-permute-start(f32[128,256]{1,0:T(8,128)} %bitcast.7), channel_id=1, source_target_pairs={{0,4},{1,5},{2,6},{3,7},{4,0},{5,1},{6,2},{7,3},{8,12},{9,13},{10,... | collective-permute-start | bytes 393224 | tf_op jit(solution)/shard_map/ppermute | solution.py:181
  6.2 8.9 %collective-permute-start.3 = (f32[128,256]{1,0:T(8,128)}, f32[128,256]{1,0:T(8,128)S(1)}, u32[]{:S(2)}, u32[]{:S(2)}) collective-permute-start(f32[128,256]{1,0:T(8,128)} %bitcast.8), channel_id=1, source_target_pairs={{0,2},{1,3},{2,0},{3,1},{4,6},{5,7},{6,4},{7,5},{8,10},{9,11},{10,... | collective-permute-start | bytes 393224 | tf_op jit(solution)/shard_map/ppermute | solution.py:181
  7.8 7.4 %collective-permute-start = (f32[128,256]{1,0:T(8,128)}, f32[128,256]{1,0:T(8,128)S(1)}, u32[]{:S(2)}, u32[]{:S(2)}) collective-permute-start(f32[128,256]{1,0:T(8,128)} %bitcast.9), channel_id=1, source_target_pairs={{0,1},{1,0},{2,3},{3,2},{4,5},{5,4},{6,7},{7,6},{8,9},{9,8},{10,11... | collective-permute-start | bytes 393224 | tf_op jit(solution)/shard_map/ppermute | solution.py:181
  7.8 9.8 %collective-permute-start.6 = (f32[256,256]{1,0:T(8,128)}, f32[256,256]{1,0:T(8,128)S(1)}, u32[]{:S(2)}, u32[]{:S(2)}) collective-permute-start(f32[256,256]{1,0:T(8,128)} %bitcast.5), channel_id=1, source_target_pairs={{0,16},{1,9},{2,18},{3,11},{4,20},{5,13},{6,22},{7,15},{8,24},{9,1... | collective-permute-start | bytes 786440 | tf_op jit(solution)/shard_map/ppermute | solution.py:181
  9.3 8.3 %collective-permute-start.7 = (f32[256,256]{1,0:T(8,128)S(1)}, f32[256,256]{1,0:T(8,128)S(1)}, u32[]{:S(2)}, u32[]{:S(2)}) collective-permute-start(f32[256,256]{1,0:T(8,128)S(1)} %collective-permute-done.5.refs_9_), channel_id=1, source_target_pairs={{0,16},{1,9},{2,18},{3,11},{4,20},{5,13},{6,22},{7,15},{8,24},{9,1... | collective-permute-start | bytes 786440 | tf_op jit(solution)/shard_map/ppermute | solution.py:181
  12.6 5.0 %collective-permute-start.8 = (f32[128,256]{1,0:T(8,128)S(1)}, f32[128,256]{1,0:T(8,128)S(1)}, u32[]{:S(2)}, u32[]{:S(2)}) collective-permute-start(f32[128,256]{1,0:T(8,128)S(1)} %collective-permute-done.1.refs_3_), channel_id=1, source_target_pairs={{0,2},{1,3},{2,0},{3,1},{4,6},{5,7},{6,4},{7,5},{8,10},{9,11},{10,... | collective-permute-start | bytes 393224 | tf_op jit(solution)/shard_map/ppermute | solution.py:181
  15.1 2.5 %collective-permute-start.2 = (f32[128,256]{1,0:T(8,128)S(1)}, f32[128,256]{1,0:T(8,128)S(1)}, u32[]{:S(2)}, u32[]{:S(2)}) collective-permute-start(f32[128,256]{1,0:T(8,128)S(1)} %collective-permute-done.1.refs_3_), channel_id=1, source_target_pairs={{0,1},{1,0},{2,3},{3,2},{4,5},{5,4},{6,7},{7,6},{8,9},{9,8},{10,11... | collective-permute-start | bytes 393224 | tf_op jit(solution)/shard_map/ppermute | solution.py:181
  15.2 2.4 %collective-permute-start.4 = (f32[128,256]{1,0:T(8,128)S(1)}, f32[128,256]{1,0:T(8,128)S(1)}, u32[]{:S(2)}, u32[]{:S(2)}) collective-permute-start(f32[128,256]{1,0:T(8,128)S(1)} %collective-permute-done.3.refs_5_), channel_id=1, source_target_pairs={{0,1},{1,0},{2,3},{3,2},{4,5},{5,4},{6,7},{7,6},{8,9},{9,8},{10,11... | collective-permute-start | bytes 393224 | tf_op jit(solution)/shard_map/ppermute | solution.py:181
  17.6 1.3 %collective-permute-start.9 = (f32[128,256]{1,0:T(8,128)S(1)}, f32[128,256]{1,0:T(8,128)S(1)}, u32[]{:S(2)}, u32[]{:S(2)}) collective-permute-start(f32[128,256]{1,0:T(8,128)S(1)} %collective-permute-done.8.refs_5_), channel_id=1, source_target_pairs={{0,1},{1,0},{2,3},{3,2},{4,5},{5,4},{6,7},{7,6},{8,9},{9,8},{10,11... | collective-permute-start | bytes 393224 | tf_op jit(solution)/shard_map/ppermute | solution.py:181
  19.6 7.3 %collective-permute-start.10 = (f32[256,128]{1,0:T(8,128)S(1)}, f32[256,128]{1,0:T(8,128)S(1)}, u32[]{:S(2)}, u32[]{:S(2)}) collective-permute-start(f32[256,128]{1,0:T(8,128)S(1)} %get-tuple-element.28), channel_id=1, source_target_pairs={{0,24},{1,25},{2,26},{3,27},{4,28},{5,29},{6,30},{7,31},{8,16},{9,... | collective-permute-start | bytes 393224 | tf_op jit(solution)/shard_map/ppermute | solution.py:181
  21.1 7.8 %collective-permute-start.11 = (f32[256,128]{1,0:T(8,128)S(1)}, f32[256,128]{1,0:T(8,128)S(1)}, u32[]{:S(2)}, u32[]{:S(2)}) collective-permute-start(f32[256,128]{1,0:T(8,128)S(1)} %get-tuple-element.28), channel_id=1, source_target_pairs={{0,16},{1,17},{2,18},{3,19},{4,20},{5,21},{6,22},{7,23},{8,24},{9,... | collective-permute-start | bytes 393224 | tf_op jit(solution)/shard_map/ppermute | solution.py:181
  23.0 5.9 %collective-permute-start.12 = (f32[256,128]{1,0:T(8,128)S(1)}, f32[256,128]{1,0:T(8,128)S(1)}, u32[]{:S(2)}, u32[]{:S(2)}) collective-permute-start(f32[256,128]{1,0:T(8,128)S(1)} %get-tuple-element.28), channel_id=1, source_target_pairs={{0,8},{1,9},{2,10},{3,11},{4,12},{5,13},{6,14},{7,15},{8,0},{9,1},... | collective-permute-start | bytes 393224 | tf_op jit(solution)/shard_map/ppermute | solution.py:181
  23.2 5.8 %copy-start = (f32[256,128]{1,0:T(8,128)S(1)}, f32[256,128]{1,0:T(8,128)}, u32[]{:S(2)}) copy-start(f32[256,128]{1,0:T(8,128)} %param.7) | copy-start | bytes 393220
